TPU v7x, 256 devices: a whole 4x4x8 slice. The times are simulated.
256 devices in a mesh: grp: 16 (over x_lo, z), bf: 16 (over x_hi, y, core).
Axes of the slice: x: 4 (x_hi: 2, x_lo: 2; x = x_hi * 2 + x_lo), y: 4, z: 8, core: 2. Of those that a mesh axis runs over, the one named last changes fastest.
Arguments:
- field: float32 [16, 524288], P(None, ('grp', 'bf')), may hold values from -6 to 6
- leaf_inverse: bfloat16 [1024, 512, 512], P(('grp', 'bf')), may hold values from -0.25 to 0.25
- col_factor: bfloat16 [2, 64, 524288], P(None, None, ('grp', 'bf')), may hold values from -0.125 to 0.125
- row_factor: bfloat16 [2, 64, 524288], P(None, None, ('grp', 'bf')), may hold values from -0.75 to 0.75
- mixing: bfloat16 [256, 2, 4, 2, 64, 64], P(('grp', 'bf')), may hold values from -0.5 to 0.5
- row_owner: int32 [2, 16], replicated, may hold values from 0 to 15, as said below
- rank_perm: int32 [2, 64], replicated, may hold values from 0 to 63, each once within a row
Outputs:
- applied: float32 [16, 524288], P(None, ('grp', 'bf'))
Inputs may be any that keep to these rules, and one draw needn't show every extreme that they name: row_owner[l, g] = (g + s_l) mod 16; one level has s_l = 8 and the other s_l = 15, which level takes which drawn from the seed.
All inputs are finite; a program needn't handle non-finite values.
Results may differ from a plain program's by a relative error of at most 0.004.
Values sent between devices are 32-bit elements; how exact they have to be, the bound alone decides.
A program may use at most 64 MiB of HBM per device.

v0:
```python
import jax
import jax.numpy as jnp
from jax import lax
from jax.sharding import PartitionSpec as P


def partner(value, axis, distance):
    mask = 2**distance
    pairs = [(source, source ^ mask) for source in range(lax.axis_size(axis))]
    return lax.ppermute(value, axis, pairs)


def shards(field, leaf_inverse, col_factor, row_factor, mixing, row_owner, rank_perm):
    hi = lax.Precision.HIGHEST
    vectors = field.shape[0]
    rows = field.shape[1]
    order = leaf_inverse.shape[1]
    levels = col_factor.shape[0]
    sections = mixing.shape[2]
    bits = lax.axis_size("bf").bit_length() - 1
    groups = lax.axis_size("grp")
    xb = field.astype(jnp.bfloat16)
    diag = jnp.einsum(
        "rnl,nlm->rnm",
        xb.reshape(vectors, rows // order, order),
        leaf_inverse,
        preferred_element_type=jnp.float32,
    ).reshape(vectors, rows)
    projected = jnp.einsum("rn,lkn->lrk", xb, col_factor, preferred_element_type=jnp.float32)
    states = jnp.stack(
        [jnp.take(projected[level], rank_perm[level], axis=1) for level in range(levels)]
    )
    own_mats = mixing[0, :, :, 0].astype(jnp.float32)
    oth_mats = mixing[0, :, :, 1].astype(jnp.float32)
    finals = []
    for level in range(levels):
        state = states[level]
        for section in range(sections):
            other = partner(state, "bf", section % bits)
            state = jnp.dot(state, own_mats[level, section], precision=hi) + jnp.dot(
                other, oth_mats[level, section], precision=hi
            )
        finals.append(state)
    states = jnp.stack(finals)
    rank = states.astype(jnp.bfloat16)
    outputs = jnp.einsum("lrk,lkn->lrn", rank, row_factor, preferred_element_type=jnp.float32)
    segment = lax.axis_index("grp")
    owners = lax.dynamic_slice_in_dim(row_owner, segment, 1, 1)
    slots = (owners == jnp.arange(groups, dtype=jnp.int32)[None, :]).astype(jnp.float32)
    placed = jnp.einsum("lt,lrn->trn", slots, outputs, precision=hi)
    summed = lax.psum_scatter(placed, "grp", scatter_dimension=0, tiled=True)[0]
    return diag + summed


def solution(mesh):
    in_specs = (
        P(None, ("grp", "bf")),
        P(("grp", "bf"), None, None),
        P(None, None, ("grp", "bf")),
        P(None, None, ("grp", "bf")),
        P(("grp", "bf"), None, None, None, None, None),
        P(),
        P(),
    )
    out_specs = P(None, ("grp", "bf"))
    return jax.shard_map(shards, mesh=mesh, in_specs=in_specs, out_specs=out_specs, check_vma=False)
```

profile of v0, /device:TPU:8, one launch (start us, length us, event | category | flops | bytes accessed | tf_op | source)
XLA Modules:
  0.0 120.1 jit_solution(17890833863682105579)
XLA Ops:
  6.5 0.9 compare_and_fusion.1
  7.4 0.9 convert_element_type.2
  8.3 1.3 %convolution_bitcast_fusion.1 = f32[2,16,64]{2,1,0:T(8,128)S(1)} fusion(bf16[2,64,2048]{2,1,0:T(8,128)(2,1)} %param.11, bf16[16,2048]{1,0:T(8,128)(2,1)S(1)} %convert_element_type.2), kind=kOutput, calls=%fused_computation.3 | convolution fusion | flops 8388608 | bytes 598016 | tf_op jit(solution)/shard_map/rn,lkn->lrk/dot_general | solution.py:29
  9.7 0.1 copy.17
  9.8 0.6 gather_fusion
  10.4 0.1 select_bitcast_fusion.1
  10.5 0.1 collective-permute-start
  10.5 0.1 copy.18
  10.6 0.6 gather_fusion.1
  11.2 0.1 select_bitcast_fusion
  11.3 0.5 collective-permute-start.4
  11.8 1.0 slice_bitcast_fusion
  12.8 0.2 fusion.16
  13.0 0.2 fusion.12
  13.2 0.9 dynamic-slice_reduce_fusion
  14.1 0.0 collective-permute-done
  14.1 0.2 convolution_add_fusion.7
  14.3 0.1 fusion.15
  14.4 2.2 %collective-permute-start.1 = (f32[16,64]{1,0:T(8,128)S(1)}, f32[16,64]{1,0:T(8,128)S(1)}, u32[]{:S(2)}, u32[]{:S(2)}) collective-permute-start(f32[16,64]{1,0:T(8,128)S(1)} %convolution_add_fusion.7), channel_id=1, source_target_pairs={{0,2},{1,3},{2,0},{3,1},{4,6},{5,7},{6,4},{7,5},{8,10},{9,11},{10,... | collective-permute-start | bytes 12296 | tf_op jit(solution)/shard_map/ppermute | solution.py:10
  16.6 0.0 collective-permute-done.4
  16.6 0.2 convolution_add_fusion.3
  16.8 0.1 fusion.11
  17.0 1.3 %collective-permute-done.1 = f32[16,64]{1,0:T(8,128)S(1)} collective-permute-done((f32[16,64]{1,0:T(8,128)S(1)}, f32[16,64]{1,0:T(8,128)S(1)}, u32[]{:S(2)}, u32[]{:S(2)}) %collective-permute-start.1) | collective-permute-done | bytes 4128 | tf_op jit(solution)/shard_map/ppermute | solution.py:10
  18.3 0.1 convolution_add_fusion.6
  18.4 2.1 %collective-permute-start.2 = (f32[16,64]{1,0:T(8,128)S(1)}, f32[16,64]{1,0:T(8,128)S(1)}, u32[]{:S(2)}, u32[]{:S(2)}) collective-permute-start(f32[16,64]{1,0:T(8,128)S(1)} %convolution_add_fusion.6), channel_id=1, source_target_pairs={{0,4},{1,5},{2,6},{3,7},{4,0},{5,1},{6,2},{7,3},{8,12},{9,13},{10,... | collective-permute-start | bytes 12296 | tf_op jit(solution)/shard_map/ppermute | solution.py:10
  20.5 0.1 fusion.14
  20.6 0.0 collective-permute-done.5
  20.7 0.1 convolution_add_fusion.2
  20.8 1.4 %collective-permute-start.6 = (f32[16,64]{1,0:T(8,128)S(1)}, f32[16,64]{1,0:T(8,128)S(1)}, u32[]{:S(2)}, u32[]{:S(2)}) collective-permute-start(f32[16,64]{1,0:T(8,128)S(1)} %convolution_add_fusion.2), channel_id=1, source_target_pairs={{0,4},{1,5},{2,6},{3,7},{4,0},{5,1},{6,2},{7,3},{8,12},{9,13},{10,... | collective-permute-start | bytes 12296 | tf_op jit(solution)/shard_map/ppermute | solution.py:10
  22.2 0.1 fusion.10
  22.3 1.3 %collective-permute-done.2 = f32[16,64]{1,0:T(8,128)S(1)} collective-permute-done((f32[16,64]{1,0:T(8,128)S(1)}, f32[16,64]{1,0:T(8,128)S(1)}, u32[]{:S(2)}, u32[]{:S(2)}) %collective-permute-start.2) | collective-permute-done | bytes 4128 | tf_op jit(solution)/shard_map/ppermute | solution.py:10
  23.6 0.1 convolution_add_fusion.5
  23.7 2.8 %collective-permute-start.3 = (f32[16,64]{1,0:T(8,128)S(1)}, f32[16,64]{1,0:T(8,128)S(1)}, u32[]{:S(2)}, u32[]{:S(2)}) collective-permute-start(f32[16,64]{1,0:T(8,128)S(1)} %convolution_add_fusion.5), channel_id=1, source_target_pairs={{0,8},{1,9},{2,10},{3,11},{4,12},{5,13},{6,14},{7,15},{8,0},{9,1},... | collective-permute-start | bytes 12296 | tf_op jit(solution)/shard_map/ppermute | solution.py:10
  26.5 0.1 fusion.13
  26.7 0.1 convolution_add_fusion.1
  26.8 2.3 %collective-permute-start.7 = (f32[16,64]{1,0:T(8,128)S(1)}, f32[16,64]{1,0:T(8,128)S(1)}, u32[]{:S(2)}, u32[]{:S(2)}) collective-permute-start(f32[16,64]{1,0:T(8,128)S(1)} %convolution_add_fusion.1), channel_id=1, source_target_pairs={{0,8},{1,9},{2,10},{3,11},{4,12},{5,13},{6,14},{7,15},{8,0},{9,1},... | collective-permute-start | bytes 12296 | tf_op jit(solution)/shard_map/ppermute | solution.py:10
  29.1 0.1 fusion.9
  29.2 0.0 collective-permute-done.3
  29.2 0.1 fusion.3
  29.4 2.6 %collective-permute-done.7 = f32[16,64]{1,0:T(8,128)S(1)} collective-permute-done((f32[16,64]{1,0:T(8,128)S(1)}, f32[16,64]{1,0:T(8,128)S(1)}, u32[]{:S(2)}, u32[]{:S(2)}) %collective-permute-start.7) | collective-permute-done | bytes 4128 | tf_op jit(solution)/shard_map/ppermute | solution.py:10
  32.0 0.1 fusion.2
  32.1 0.2 fusion.17
  32.3 1.2 %fusion.4 = f32[16,16,2048]{2,0,1:T(8,128)S(1)} fusion(f32[2,16,2048]{2,1,0:T(8,128)S(1)} %fusion.17, s32[2]{0:T(128)S(1)} %dynamic-slice_reduce_fusion), kind=kOutput, calls=%fused_computation.16 | convolution fusion | flops 12582944 | bytes 2359304 | tf_op jit(solution)/shard_map/lt,lrn->trn/dot_general | solution.py:50
  33.5 2.6 %copy.20 = f32[16,16,2048]{2,1,0:T(8,128)} copy(f32[16,16,2048]{2,0,1:T(8,128)S(1)} %fusion.4) | data formatting | bytes 4194304 | tf_op jit(solution)/shard_map/lt,lrn->trn/dot_general | solution.py:50
  36.1 0.0 reduce-scatter.2.cloned.1.call-update
  36.1 0.4 convolution_bitcast_fusion
  36.5 75.2 %reduce-scatter.2.cloned.1.call-done = f32[1,16,2048]{2,1,0:T(8,128)} async-done(((f32[16,16,2048]{2,1,0:T(8,128)}), f32[1,16,2048]{2,1,0:T(8,128)}) %reduce-scatter.2.cloned.1.call-update) | async-done | bytes 131088 | tf_op jit(solution)/shard_map/reduce_scatter | solution.py:51
  111.7 1.6 %bitcast_add_fusion = f32[16,2048]{1,0:T(8,128)} fusion(f32[16,2048]{1,0:T(8,128)S(1)} %bitcast.108, f32[1,16,2048]{2,1,0:T(8,128)} %reduce-scatter.2.cloned.1.call-done), kind=kLoop, calls=%fused_computation.18 | loop fusion | flops 32768 | bytes 393216 | tf_op jit(solution)/shard_map/add | solution.py:52
  (11 shorter events, 0.1 us)
Async XLA Ops:
  6.5 29.6 %copy-start = (bf16[4,512,512]{2,1,0:T(8,128)(2,1)S(1)}, bf16[4,512,512]{2,1,0:T(8,128)(2,1)}, u32[]{:S(2)}) copy-start(bf16[4,512,512]{2,1,0:T(8,128)(2,1)} %param.10) | copy-start | bytes 6291460
  6.5 25.6 %copy-start.1 = (bf16[2,64,2048]{2,1,0:T(8,128)(2,1)S(1)}, bf16[2,64,2048]{2,1,0:T(8,128)(2,1)}, u32[]{:S(2)}) copy-start(bf16[2,64,2048]{2,1,0:T(8,128)(2,1)} %param.12) | copy-start | bytes 1572868
  6.5 105.2 %reduce-scatter.2.cloned.1.call-start = ((), (), s32[]{:S(2)}) async-start(), calls=%async_computation.1 | async-start | bytes 2228224 | tf_op jit(solution)/shard_map/reduce_scatter | solution.py:51
  10.5 3.7 %collective-permute-start = (f32[16,64]{0,1:T(8,128)S(1)}, f32[16,64]{0,1:T(8,128)S(1)}, u32[]{:S(2)}, u32[]{:S(2)}) collective-permute-start(f32[16,64]{0,1:T(8,128)S(1)} %select_bitcast_fusion.1), channel_id=1, source_target_pairs={{0,1},{1,0},{2,3},{3,2},{4,5},{5,4},{6,7},{7,6},{8,9},{9,8},{10,11... | collective-permute-start | bytes 12296 | tf_op jit(solution)/shard_map/ppermute | solution.py:10
  11.3 5.4 %collective-permute-start.4 = (f32[16,64]{0,1:T(8,128)S(1)}, f32[16,64]{0,1:T(8,128)S(1)}, u32[]{:S(2)}, u32[]{:S(2)}) collective-permute-start(f32[16,64]{0,1:T(8,128)S(1)} %select_bitcast_fusion), channel_id=1, source_target_pairs={{0,1},{1,0},{2,3},{3,2},{4,5},{5,4},{6,7},{7,6},{8,9},{9,8},{10,11... | collective-permute-start | bytes 12296 | tf_op jit(solution)/shard_map/ppermute | solution.py:10
  14.4 3.8 %collective-permute-start.1 = (f32[16,64]{1,0:T(8,128)S(1)}, f32[16,64]{1,0:T(8,128)S(1)}, u32[]{:S(2)}, u32[]{:S(2)}) collective-permute-start(f32[16,64]{1,0:T(8,128)S(1)} %convolution_add_fusion.7), channel_id=1, source_target_pairs={{0,2},{1,3},{2,0},{3,1},{4,6},{5,7},{6,4},{7,5},{8,10},{9,11},{10,... | collective-permute-start | bytes 12296 | tf_op jit(solution)/shard_map/ppermute | solution.py:10
  17.0 3.7 %collective-permute-start.5 = (f32[16,64]{1,0:T(8,128)S(1)}, f32[16,64]{1,0:T(8,128)S(1)}, u32[]{:S(2)}, u32[]{:S(2)}) collective-permute-start(f32[16,64]{1,0:T(8,128)S(1)} %convolution_add_fusion.3), channel_id=1, source_target_pairs={{0,2},{1,3},{2,0},{3,1},{4,6},{5,7},{6,4},{7,5},{8,10},{9,11},{10,... | collective-permute-start | bytes 12296 | tf_op jit(solution)/shard_map/ppermute | solution.py:10
  18.4 5.2 %collective-permute-start.2 = (f32[16,64]{1,0:T(8,128)S(1)}, f32[16,64]{1,0:T(8,128)S(1)}, u32[]{:S(2)}, u32[]{:S(2)}) collective-permute-start(f32[16,64]{1,0:T(8,128)S(1)} %convolution_add_fusion.6), channel_id=1, source_target_pairs={{0,4},{1,5},{2,6},{3,7},{4,0},{5,1},{6,2},{7,3},{8,12},{9,13},{10,... | collective-permute-start | bytes 12296 | tf_op jit(solution)/shard_map/ppermute | solution.py:10
  20.8 5.9 %collective-permute-start.6 = (f32[16,64]{1,0:T(8,128)S(1)}, f32[16,64]{1,0:T(8,128)S(1)}, u32[]{:S(2)}, u32[]{:S(2)}) collective-permute-start(f32[16,64]{1,0:T(8,128)S(1)} %convolution_add_fusion.2), channel_id=1, source_target_pairs={{0,4},{1,5},{2,6},{3,7},{4,0},{5,1},{6,2},{7,3},{8,12},{9,13},{10,... | collective-permute-start | bytes 12296 | tf_op jit(solution)/shard_map/ppermute | solution.py:10
  23.7 5.5 %collective-permute-start.3 = (f32[16,64]{1,0:T(8,128)S(1)}, f32[16,64]{1,0:T(8,128)S(1)}, u32[]{:S(2)}, u32[]{:S(2)}) collective-permute-start(f32[16,64]{1,0:T(8,128)S(1)} %convolution_add_fusion.5), channel_id=1, source_target_pairs={{0,8},{1,9},{2,10},{3,11},{4,12},{5,13},{6,14},{7,15},{8,0},{9,1},... | collective-permute-start | bytes 12296 | tf_op jit(solution)/shard_map/ppermute | solution.py:10
  26.8 5.2 %collective-permute-start.7 = (f32[16,64]{1,0:T(8,128)S(1)}, f32[16,64]{1,0:T(8,128)S(1)}, u32[]{:S(2)}, u32[]{:S(2)}) collective-permute-start(f32[16,64]{1,0:T(8,128)S(1)} %convolution_add_fusion.1), channel_id=1, source_target_pairs={{0,8},{1,9},{2,10},{3,11},{4,12},{5,13},{6,14},{7,15},{8,0},{9,1},... | collective-permute-start | bytes 12296 | tf_op jit(solution)/shard_map/ppermute | solution.py:10
Sparse Core Ops, SparseCore 0:
  36.2 75.4 reduce-scatter.1
where the time goes:
time: 120 us
  waiting for transfers between devices  80.4 us (67%)
  between operations  13.5 us (11%)
  starting transfers between devices  11.5 us (10%)
  local copies, waits for them, and re-layouts  5.83 us (5%)
  matrix products  5.39 us (4%)
  other arithmetic  3.51 us (3%)
    reduce_scatter x1, waiting for transfers between devices, shards(): summed = lax.psum_scatter(placed, 'grp', scatter_dimension=0, tiled=True)[0]  75.2 us
    ppermute x8, starting transfers between devices, partner(): return lax.ppermute(value, axis, pairs)  11.5 us
    ppermute x8, waiting for transfers between devices, partner(): return lax.ppermute(value, axis, pairs)  5.18 us
    dot_general x1, local copies, waits for them, and re-layouts, shards(): placed = jnp.einsum('lt,lrn->trn', slots, outputs, precision=hi)  2.55 us
  transfers between devices with their start and end apart: 9, of which 4 were waited for; matrix products, arithmetic and copies ran while one was open for 4% of the time, Pallas kernels for 0%

commit v1 on v0

v1 whole, which is shorter than its diff:
```python
import functools

import jax
import jax.numpy as jnp
from jax import lax
from jax.experimental import pallas as pl
from jax.experimental.pallas import tpu as pltpu
from jax.sharding import PartitionSpec as P

MESH = pl.DeviceIdType.MESH
CHUNKS = 4


def split_dot(lhs, weights):
    high = lhs.astype(jnp.bfloat16)
    low = (lhs - high.astype(jnp.float32)).astype(jnp.bfloat16)
    both = jnp.dot(
        jnp.concatenate([high, low], axis=0), weights, preferred_element_type=jnp.float32
    )
    rows = lhs.shape[0]
    return both[:rows] + both[rows:]


def kernel(
    field_hbm, leaf_hbm, col_hbm, row_hbm, mix_hbm, owner_ref, perm_ref,
    out_ref,
    field, leaf, col, row, mix, weights, own, other, outgoing, incoming,
    load_sem, leaf_sem, send_sem, recv_sem, shift_send, shift_recv,
):
    groups, width = lax.axis_size("grp"), lax.axis_size("bf")
    g, b = lax.axis_index("grp"), lax.axis_index("bf")
    vectors, rows = field.shape
    levels, rank, _ = col.shape
    leaves, order, _ = leaf.shape
    sections = mix.shape[2]
    bits = width.bit_length() - 1
    both = levels * rank

    loads = [
        pltpu.make_async_copy(src, dst, load_sem.at[i])
        for i, (src, dst) in enumerate(
            ((field_hbm, field), (col_hbm, col), (mix_hbm, mix), (row_hbm, row))
        )
    ]
    for copy in loads:
        copy.start()
    leaf_loads = [
        pltpu.make_async_copy(leaf_hbm.at[n], leaf.at[n], leaf_sem.at[n]) for n in range(leaves)
    ]
    for copy in leaf_loads:
        copy.start()

    partners = []
    for bit in range(bits):
        step = 2**bit
        partners.append(b + step - 2 * step * ((b // step) % 2))
    half = (g + groups // 2) % groups
    down, up = (g + groups - 1) % groups, (g + 1) % groups
    barrier = pltpu.get_barrier_semaphore()
    friends = [(g, p) for p in partners] + [(half, b), (down, b), (up, b)]
    for friend in friends:
        pl.semaphore_signal(barrier, inc=1, device_id=friend, device_id_type=MESH)

    loads[0].wait()
    loads[1].wait()
    xb = field[...].astype(jnp.bfloat16)
    own[0] = lax.dot_general(
        xb, col[...].reshape(both, rows), (((1,), (1,)), ((), ())),
        preferred_element_type=jnp.float32,
    )
    pl.semaphore_wait(barrier, len(friends))

    def exchange(section):
        return pltpu.make_async_remote_copy(
            src_ref=own.at[section], dst_ref=other.at[section],
            send_sem=send_sem.at[section], recv_sem=recv_sem.at[section],
            device_id=(g, partners[section % bits]), device_id_type=MESH,
        )

    def diagonal(n):
        leaf_loads[n].wait()
        out_ref[:, n * order:(n + 1) * order] = jnp.dot(
            xb[:, n * order:(n + 1) * order], leaf[n], preferred_element_type=jnp.float32
        )

    copy = exchange(0)
    copy.start()
    loads[2].wait()
    zero = jnp.zeros((rank, rank), jnp.bfloat16)
    for level in range(levels):
        index = lax.broadcasted_iota(jnp.int32, (rank, rank), 0)
        chosen = jnp.where(index == perm_ref[level:level + 1, :], 1.0, 0.0).astype(jnp.bfloat16)
        for section in range(sections):
            for part in range(2):
                block = mix[0, level, section, part]
                if section == 0:
                    block = jnp.dot(chosen, block, preferred_element_type=jnp.float32).astype(jnp.bfloat16)
                line = [zero] * levels
                line[level] = block
                start = part * both + level * rank
                weights[section, start:start + rank, :] = jnp.concatenate(line, axis=1)
    for section in range(sections):
        if section < leaves:
            diagonal(section)
        copy.wait()
        state = split_dot(
            jnp.concatenate([own[section], other[section]], axis=1), weights[section]
        )
        if section + 1 < sections:
            own[section + 1] = state
            copy = exchange(section + 1)
            copy.start()
    for n in range(sections, leaves):
        diagonal(n)

    level_of = lax.broadcasted_iota(jnp.int32, (vectors, both), 1) // rank
    half_level = jnp.where(owner_ref[0, 0] == groups // 2, 0, 1)
    pair = jnp.concatenate(
        [jnp.where(level_of == half_level, state, 0.0), jnp.where(level_of == half_level, 0.0, state)],
        axis=0,
    ).astype(jnp.bfloat16)
    loads[3].wait()
    factor = row[...].reshape(both, rows)
    size = rows // CHUNKS
    copies = []
    for c in range(CHUNKS):
        sent = jnp.dot(pair, factor[:, c * size:(c + 1) * size], preferred_element_type=jnp.float32)
        for way, target in enumerate((half, down)):
            outgoing[way, c] = sent[way * vectors:(way + 1) * vectors]
            copy = pltpu.make_async_remote_copy(
                src_ref=outgoing.at[way, c], dst_ref=incoming.at[way, c],
                send_sem=shift_send.at[way, c], recv_sem=shift_recv.at[way, c],
                device_id=(target, b), device_id_type=MESH,
            )
            copy.start()
            copies.append(copy)
    for c in range(CHUNKS):
        copies[2 * c].wait_recv()
        copies[2 * c + 1].wait_recv()
        out_ref[:, c * size:(c + 1) * size] += incoming[0, c] + incoming[1, c]
    for copy in copies:
        copy.wait_send()


def shards(field, leaf_inverse, col_factor, row_factor, mixing, row_owner, rank_perm):
    vectors, rows = field.shape
    levels, rank, _ = col_factor.shape
    sections = mixing.shape[2]
    both = levels * rank
    f32, bf16 = jnp.float32, jnp.bfloat16
    hbm = pl.BlockSpec(memory_space=pltpu.HBM)
    vmem = pl.BlockSpec(memory_space=pltpu.VMEM)
    smem = pl.BlockSpec(memory_space=pltpu.SMEM)
    return pl.pallas_call(
        kernel,
        out_shape=jax.ShapeDtypeStruct((vectors, rows), f32),
        in_specs=[hbm, hbm, hbm, hbm, hbm, smem, vmem],
        out_specs=vmem,
        scratch_shapes=[
            pltpu.VMEM(field.shape, f32),
            pltpu.VMEM(leaf_inverse.shape, bf16),
            pltpu.VMEM(col_factor.shape, bf16),
            pltpu.VMEM(row_factor.shape, bf16),
            pltpu.VMEM(mixing.shape, bf16),
            pltpu.VMEM((sections, 2 * both, both), bf16),
            pltpu.VMEM((sections, vectors, both), f32),
            pltpu.VMEM((sections, vectors, both), f32),
            pltpu.VMEM((2, CHUNKS, vectors, rows // CHUNKS), f32),
            pltpu.VMEM((2, CHUNKS, vectors, rows // CHUNKS), f32),
            pltpu.SemaphoreType.DMA((4,)),
            pltpu.SemaphoreType.DMA((leaf_inverse.shape[0],)),
            pltpu.SemaphoreType.DMA((sections,)),
            pltpu.SemaphoreType.DMA((sections,)),
            pltpu.SemaphoreType.DMA((2, CHUNKS)),
            pltpu.SemaphoreType.DMA((2, CHUNKS)),
        ],
        compiler_params=pltpu.CompilerParams(
            collective_id=0, has_side_effects=True, vmem_limit_bytes=60 * 2**20
        ),
    )(field, leaf_inverse, col_factor, row_factor, mixing, row_owner, rank_perm)


def solution(mesh):
    in_specs = (
        P(None, ("grp", "bf")),
        P(("grp", "bf"), None, None),
        P(None, None, ("grp", "bf")),
        P(None, None, ("grp", "bf")),
        P(("grp", "bf"), None, None, None, None, None),
        P(),
        P(),
    )
    out_specs = P(None, ("grp", "bf"))
    return jax.shard_map(shards, mesh=mesh, in_specs=in_specs, out_specs=out_specs, check_vma=False)
```

time: 120 us -> 27.4 us (0.23)
  the two profiles are of different devices: /device:TPU:8 before, /device:TPU:2 now
where the time goes in v1:
time: 27.4 us; the launch traced here: 27.2 us
  Pallas kernels  25.7 us (94%)
  local copies, waits for them, and re-layouts  1.57 us (6%)
    pallas_call x1, Pallas kernels, shards(): pl.pallas_call(kernel, out_shape=jax.ShapeDtypeStruct((vectors, rows), f3...  25.7 us
    unnamed x1, local copies, waits for them, and re-layouts  1.57 us

profile of v1, /device:TPU:2, one launch (start us, length us, event | category | flops | bytes accessed | tf_op | source)
XLA Modules:
  0.0 27.2 jit_solution(14496727682517117693)
XLA Ops:
  0.0 25.7 %shard_map.73 = f32[16,2048]{1,0:T(8,128)} custom-call(f32[16,2048]{1,0:T(8,128)} %field_hbm.1, bf16[4,512,512]{2,1,0:T(8,128)(2,1)} %leaf_hbm.1, bf16[2,64,2048]{2,1,0:T(8,128)(2,1)} %col_hbm.1, bf16[2,64,2048]{2,1,0:T(8,128)(2,1)} %row_hbm.1, bf16[1,2,4,2,64,64]{5,4,3,2,1,0:T(8,128)(2,1)} %mix_hbm.1, s32[2,16]{1,0:T(2,128)} %owner_ref.1, s32[2,64]{1,0:T(2,128)} %perm_ref.1), custom_call_target="tpu_custom_call" | custom-call | tf_op jit(solution)/shard_map/pallas_call | solution.py:154
  25.7 1.6 %copy.9 = f32[16,2048]{1,0:T(8,128)} copy(f32[16,2048]{1,0:T(8,128)} %shard_map.73) | data formatting | bytes 262144

commit v2 on v1

v2 whole, which is shorter than its diff:
```python
import jax
import jax.numpy as jnp
from jax import lax
from jax.experimental import pallas as pl
from jax.experimental.pallas import tpu as pltpu
from jax.sharding import PartitionSpec as P

MESH = pl.DeviceIdType.MESH
CHUNKS = 4


def split_dot(lhs, weights):
    high = lhs.astype(jnp.bfloat16)
    low = (lhs - high.astype(jnp.float32)).astype(jnp.bfloat16)
    both = jnp.dot(
        jnp.concatenate([high, low], axis=0), weights, preferred_element_type=jnp.float32
    )
    rows = lhs.shape[0]
    return both[:rows] + both[rows:]


def flip(index, bit):
    step = 2**bit
    return index + step - 2 * step * ((index // step) % 2)


def kernel(
    field_hbm, leaf_hbm, col_hbm, row_hbm, mix_hbm, owner_hbm, perm_hbm,
    out_ref,
    field, leaf, col, row, mix, owner, perm, weights, lent, borrowed, mail, box, outgoing, incoming,
    load_sem, leaf_sem, lend_sem, mail_send, mail_recv, shift_send, shift_recv,
):
    g, b = lax.axis_index("grp"), lax.axis_index("bf")
    groups = lax.axis_size("grp")
    vectors, rows = field.shape
    levels, rank, _ = col.shape
    leaves, order, _ = leaf.shape
    sections = mix.shape[2]
    both = levels * rank

    def load(i, src, dst):
        copy = pltpu.make_async_copy(src, dst, load_sem.at[i])
        copy.start()
        return copy

    field_load = load(0, field_hbm, field)
    col_load = load(1, col_hbm, col)
    perm_load = load(2, perm_hbm, perm)
    mix_load = load(3, mix_hbm, mix)
    row_load = load(4, row_hbm, row)
    owner_load = load(5, owner_hbm, owner)
    leaf_loads = [
        pltpu.make_async_copy(leaf_hbm.at[n], leaf.at[n], leaf_sem.at[n]) for n in range(leaves)
    ]
    for copy in leaf_loads:
        copy.start()

    line, z = groups // 2, g % (groups // 2)
    half = (g + line) % groups
    down = g - z + (z + line - 1) % line
    up = g - z + (z + 1) % line
    first, second, third, fourth = (flip(b, bit) for bit in range(4))
    cross = flip(second, 2)
    friends = [(g, p) for p in (first, second, third, fourth, cross)]
    friends += [(half, b), (down, b), (up, b)]
    barrier = pltpu.get_barrier_semaphore()
    for friend in friends:
        pl.semaphore_signal(barrier, inc=1, device_id=friend, device_id_type=MESH)

    def post(slot, target):
        copy = pltpu.make_async_remote_copy(
            src_ref=mail.at[slot], dst_ref=box.at[slot],
            send_sem=mail_send.at[slot], recv_sem=mail_recv.at[slot],
            device_id=(g, target), device_id_type=MESH,
        )
        copy.start()
        return copy

    def diagonal(n):
        leaf_loads[n].wait()
        out_ref[:, n * order:(n + 1) * order] = jnp.dot(
            xb[:, n * order:(n + 1) * order], leaf[n], preferred_element_type=jnp.float32
        )

    zero = jnp.zeros((rank, rank), jnp.bfloat16)

    def blocks(index, part, made):
        for level in range(levels):
            line = [zero] * levels
            line[level] = made(level)
            start = part * both + level * rank
            weights[index, start:start + rank, :] = jnp.concatenate(line, axis=1)

    def factors(section, part):
        blocks(section, part, lambda level: mix[0, level, section, part])

    field_load.wait()
    col_load.wait()
    xb = field[...].astype(jnp.bfloat16)
    mail[0] = lax.dot_general(
        xb, col[...].reshape(both, rows), (((1,), (1,)), ((), ())),
        preferred_element_type=jnp.float32,
    )
    mix_load.wait()
    lent[...] = jnp.concatenate([mix[0, level, 1, 1] for level in range(levels)], axis=1).astype(jnp.float32)
    pl.semaphore_wait(barrier, len(friends))
    start = post(0, first)
    loan = pltpu.make_async_remote_copy(
        src_ref=lent, dst_ref=borrowed, send_sem=lend_sem.at[0], recv_sem=lend_sem.at[1],
        device_id=(g, second), device_id_type=MESH,
    )
    loan.start()
    perm_load.wait()
    index = lax.broadcasted_iota(jnp.int32, (rank, rank), 0)
    for part in range(2):
        blocks(0, part, lambda level: jnp.dot(
            jnp.where(index == perm[level:level + 1, :], 1.0, 0.0).astype(jnp.bfloat16),
            mix[0, level, 0, part], preferred_element_type=jnp.float32,
        ).astype(jnp.bfloat16))
    factors(1, 0)
    start.wait_recv()
    state = split_dot(jnp.concatenate([mail[0], box[0]], axis=1), weights[0])

    mail[1] = state
    raw = post(1, second)
    mine = split_dot(state, weights[1, :both])
    mail[2] = mine
    direct = post(2, third)
    factors(1, 1)
    factors(2, 0)
    factors(2, 1)
    loan.wait_recv()
    blocks(sections, 0, lambda level: borrowed[:, level * rank:(level + 1) * rank].astype(jnp.bfloat16))
    mail[3] = split_dot(state, weights[sections, :both])
    detour = post(3, cross)
    factors(3, 0)
    factors(3, 1)
    diagonal(0)
    diagonal(1)
    raw.wait_recv()
    state = mine + split_dot(box[1], weights[1, both:])
    mine = split_dot(state, weights[2, :both])
    detour.wait_recv()
    direct.wait_recv()
    state = mine + split_dot(box[2] + box[3], weights[2, both:])

    mail[4] = state
    last = post(4, fourth)
    mine = split_dot(state, weights[3, :both])
    for n in range(2, leaves):
        diagonal(n)
    row_load.wait()
    owner_load.wait()
    level_of = lax.broadcasted_iota(jnp.int32, (vectors, both), 1) // rank
    half_level = jnp.where(owner[0:1, 0:1] == line, 0, 1)
    to_half = level_of == half_level
    last.wait_recv()
    state = mine + split_dot(box[4], weights[3, both:])

    pair = jnp.concatenate(
        [jnp.where(to_half, state, 0.0), jnp.where(to_half, 0.0, state)], axis=0
    ).astype(jnp.bfloat16)
    factor = row[...].reshape(both, rows)
    size = rows // CHUNKS

    def shift(way, c):
        return pltpu.make_async_remote_copy(
            src_ref=outgoing.at[way, c], dst_ref=incoming.at[way, c],
            send_sem=shift_send.at[way, c], recv_sem=shift_recv.at[way, c],
            device_id=((half, down)[way], b), device_id_type=MESH,
        )

    for c in range(CHUNKS):
        sent = jnp.dot(pair, factor[:, c * size:(c + 1) * size], preferred_element_type=jnp.float32)
        outgoing[0, c] = sent[:vectors]
        outgoing[1, c] = sent[vectors:]
        shift(1, c).start()

        @pl.when(z != line - 1)
        def _():
            shift(0, c).start()

    @pl.when(z == line - 1)
    def _():
        for c in range(CHUNKS):
            shift(1, c).wait_recv()
            outgoing[0, c] += incoming[1, c]
            shift(0, c).start()

    for c in range(CHUNKS):
        where = slice(c * size, (c + 1) * size)
        shift(0, c).wait_recv()

        @pl.when(z == line - 1)
        def _():
            out_ref[:, where] += incoming[0, c]

        @pl.when(z != line - 1)
        def _():
            shift(1, c).wait_recv()
            out_ref[:, where] += incoming[0, c] + incoming[1, c]

    for copy in (start, loan, raw, direct, detour, last):
        copy.wait_send()
    for c in range(CHUNKS):
        for way in range(2):
            shift(way, c).wait_send()


def shards(field, leaf_inverse, col_factor, row_factor, mixing, row_owner, rank_perm):
    vectors, rows = field.shape
    levels, rank, _ = col_factor.shape
    sections = mixing.shape[2]
    both = levels * rank
    f32, bf16 = jnp.float32, jnp.bfloat16
    args = (field, leaf_inverse, col_factor, row_factor, mixing, row_owner, rank_perm)
    args = [pltpu.with_memory_space_constraint(x, pltpu.HBM) for x in args]
    return pl.pallas_call(
        kernel,
        out_shape=pltpu.VMEM((vectors, rows), f32),
        in_specs=[pl.BlockSpec(memory_space=pltpu.HBM)] * len(args),
        out_specs=pl.BlockSpec(memory_space=pltpu.VMEM),
        scratch_shapes=[
            pltpu.VMEM(field.shape, f32),
            pltpu.VMEM(leaf_inverse.shape, bf16),
            pltpu.VMEM(col_factor.shape, bf16),
            pltpu.VMEM(row_factor.shape, bf16),
            pltpu.VMEM(mixing.shape, bf16),
            pltpu.VMEM(row_owner.shape, jnp.int32),
            pltpu.VMEM(rank_perm.shape, jnp.int32),
            pltpu.VMEM((sections + 1, 2 * both, both), bf16),
            pltpu.VMEM((rank, both), f32),
            pltpu.VMEM((rank, both), f32),
            pltpu.VMEM((5, vectors, both), f32),
            pltpu.VMEM((5, vectors, both), f32),
            pltpu.VMEM((2, CHUNKS, vectors, rows // CHUNKS), f32),
            pltpu.VMEM((2, CHUNKS, vectors, rows // CHUNKS), f32),
            pltpu.SemaphoreType.DMA((6,)),
            pltpu.SemaphoreType.DMA((leaf_inverse.shape[0],)),
            pltpu.SemaphoreType.DMA((2,)),
            pltpu.SemaphoreType.DMA((5,)),
            pltpu.SemaphoreType.DMA((5,)),
            pltpu.SemaphoreType.DMA((2, CHUNKS)),
            pltpu.SemaphoreType.DMA((2, CHUNKS)),
        ],
        compiler_params=pltpu.CompilerParams(
            collective_id=0, has_side_effects=True, vmem_limit_bytes=60 * 2**20
        ),
    )(*args)


def solution(mesh):
    in_specs = (
        P(None, ("grp", "bf")),
        P(("grp", "bf"), None, None),
        P(None, None, ("grp", "bf")),
        P(None, None, ("grp", "bf")),
        P(("grp", "bf"), None, None, None, None, None),
        P(),
        P(),
    )
    out_specs = P(None, ("grp", "bf"))
    return jax.shard_map(shards, mesh=mesh, in_specs=in_specs, out_specs=out_specs, check_vma=False)
```

time: 27.4 us -> 23.1 us (0.84)
  Pallas kernels: 25.7 us -> 22.3 us
  local copies, waits for them, and re-layouts: 1.57 us -> 0.66 us
    pallas_call x1, Pallas kernels: 25.7 us -> 22.3 us  [shards(): pl.pallas_call(kernel, out_shape=pltpu.VMEM((vectors, rows), f32), in_spe...]
    unnamed x1, local copies, waits for them, and re-layouts: 1.57 us -> 0.66 us
where the time goes in v2:
time: 23.1 us; the launch traced here: 23 us
  Pallas kernels  22.3 us (97%)
  local copies, waits for them, and re-layouts  0.66 us (3%)
    pallas_call x1, Pallas kernels, shards(): pl.pallas_call(kernel, out_shape=pltpu.VMEM((vectors, rows), f32), in_spe...  22.3 us
    unnamed x1, local copies, waits for them, and re-layouts  0.66 us

profile of v2, /device:TPU:2, one launch (start us, length us, event | category | flops | bytes accessed | tf_op | source)
XLA Modules:
  0.0 23.0 jit_solution(903197176025626233)
XLA Ops:
  0.0 22.3 %shard_map.73 = f32[16,2048]{1,0:T(8,128)S(1)} custom-call(f32[16,2048]{1,0:T(8,128)} %field_hbm.1, bf16[4,512,512]{2,1,0:T(8,128)(2,1)} %leaf_hbm.1, bf16[2,64,2048]{2,1,0:T(8,128)(2,1)} %col_hbm.1, bf16[2,64,2048]{2,1,0:T(8,128)(2,1)} %row_hbm.1, bf16[1,2,4,2,64,64]{5,4,3,2,1,0:T(8,128)(2,1)} %mix_hbm.1, s32[2,16]{1,0:T(2,128)} %owner_hbm.1, s32[2,64]{1,0:T(2,128)} %perm_hbm.1), custom_call_target="tpu_custom_call" | custom-call | tf_op jit(solution)/shard_map/pallas_call | solution.py:218
  22.3 0.7 %copy.9 = f32[16,2048]{1,0:T(8,128)} copy(f32[16,2048]{1,0:T(8,128)S(1)} %shard_map.73) | data formatting | bytes 262144

commit v3 on v0

v3 whole, which is shorter than its diff:
```python
import jax
import jax.numpy as jnp
from jax import lax
from jax.experimental import pallas as pl
from jax.experimental.pallas import tpu as pltpu
from jax.sharding import PartitionSpec as P

MESH = pl.DeviceIdType.MESH
CHUNKS = 4
RAW, DIRECT, DETOUR, LAST = range(4)


def split_dot(lhs, weights):
    high = lhs.astype(jnp.bfloat16)
    low = (lhs - high.astype(jnp.float32)).astype(jnp.bfloat16)
    both = jnp.dot(
        jnp.concatenate([high, low], axis=0), weights, preferred_element_type=jnp.float32
    )
    rows = lhs.shape[0]
    return both[:rows] + both[rows:]


def flip(index, bit):
    step = 2**bit
    return index + step - 2 * step * ((index // step) % 2)


def kernel(
    field_hbm, leaf_hbm, col_hbm, row_hbm, mix_hbm, owner_hbm, perm_hbm,
    out_ref,
    field, leaf, col, row, mix, owner, perm, weights,
    seed_out, seed_in, gift_out, gift_in, lent, borrowed, mail_out, mail_in,
    word_out, word_in, rows_out, rows_in, rows_low, outgoing, incoming, relay,
    load_sem, leaf_sem, seed_sem, gift_send, gift_recv, lend_send, lend_recv, mail_send, mail_recv,
    word_send, word_recv, rows_send, rows_recv, shift_send, shift_recv, relay_send, relay_recv, ready,
):
    g, b = lax.axis_index("grp"), lax.axis_index("bf")
    groups = lax.axis_size("grp")
    vectors, rows = field.shape
    levels, rank, _ = col.shape
    leaves, order, _ = leaf.shape
    sections = mix.shape[2]
    both = levels * rank
    size = rows // CHUNKS
    f32, bf16 = jnp.float32, jnp.bfloat16

    def load(i, src, dst):
        copy = pltpu.make_async_copy(src, dst, load_sem.at[i])
        copy.start()
        return copy

    mix_load = load(3, mix_hbm, mix)
    field_load = load(0, field_hbm, field)
    col_load = load(1, col_hbm, col)
    perm_load = load(2, perm_hbm, perm)
    owner_load = load(5, owner_hbm, owner)
    row_load = load(4, row_hbm, row)
    leaf_loads = [
        pltpu.make_async_copy(leaf_hbm.at[n], leaf.at[n], leaf_sem.at[n]) for n in range(leaves)
    ]
    for copy in leaf_loads:
        copy.start()

    line, core = groups // 2, b % 2
    z = g % line
    half, down, up = (g + line) % groups, g - z + (z + line - 1) % line, g - z + (z + 1) % line
    sibling, second, third, fourth = (flip(b, bit) for bit in range(4))
    cross = flip(second, 2)
    bottom, top = z == 0, z == line - 1
    barrier = pltpu.get_barrier_semaphore()

    def greet(group, member):
        pl.semaphore_signal(barrier, inc=1, device_id=(group, member), device_id_type=MESH)

    def meet(count, below, above):
        pl.semaphore_wait(
            barrier, count + below * jnp.where(bottom, 0, 1) + above * jnp.where(top, 1, 0)
        )

    greet(g, sibling)
    greet(half, b)

    @pl.when(jnp.logical_not(top))
    def _():
        greet(up, b)

    @pl.when(bottom)
    def _():
        greet(down, b + 1 - core)

    def remote(src, dst, send, recv, group, member):
        return pltpu.make_async_remote_copy(
            src_ref=src, dst_ref=dst, send_sem=send, recv_sem=recv,
            device_id=(group, member), device_id_type=MESH,
        )

    seed = remote(seed_out, seed_in, seed_sem.at[0], seed_sem.at[1], g, sibling)
    gifts = [
        remote(gift_out.at[i], gift_in.at[i], gift_send.at[i], gift_recv.at[i], g, sibling)
        for i in range(sections)
    ]

    def lend(j, member):
        return remote(lent, borrowed.at[j], lend_send.at[0], lend_recv.at[j], g, member)

    def shift(way, c):
        return remote(
            outgoing.at[way, c], incoming.at[way, c], shift_send.at[way, c], shift_recv.at[way, c],
            (half, down)[way], b,
        )

    def inward(c, member):
        return remote(
            outgoing.at[1, c], relay.at[c], shift_send.at[1, c], relay_recv.at[c], down, member
        )

    def onward(c):
        return remote(
            relay.at[c], incoming.at[1, c], relay_send.at[c], shift_recv.at[1, c], half, sibling
        )

    def word(i, group, member):
        return remote(word_out.at[i], word_in.at[i], word_send.at[i], word_recv.at[i], group, member)

    def give_rows(way):
        return remote(
            rows_out.at[way], rows_in.at[way], rows_send.at[way], rows_recv.at[way],
            (half, down)[way], b,
        )

    def joined(section, part):
        return jnp.concatenate([mix[0, level, section, part] for level in range(levels)], axis=1)

    def project():
        field_load.wait()
        col_load.wait()
        return lax.dot_general(
            field[...].astype(bf16), col[...].reshape(both, rows), (((1,), (1,)), ((), ())),
            preferred_element_type=f32,
        )

    def diagonal(n):
        leaf_loads[n].wait()
        where = slice(n * order, (n + 1) * order)
        out_ref[:, where] = jnp.dot(
            field[:, where].astype(bf16), leaf[n], preferred_element_type=f32
        )

    @pl.when(core == 0)
    def _():
        greet(half, sibling)

        @pl.when(jnp.logical_not(top))
        def _():
            greet(up, sibling)

        mix_load.wait()
        for part in range(2):
            gift_out[0, part] = joined(0, part).astype(f32)
        lent[...] = joined(1, 1).astype(f32)
        seed_out[...] = project()
        meet(3, 1, 0)
        seed.start()
        gifts[0].start()
        loan = lend(0, flip(second, 0))
        loan.start()
        for section in range(1, sections):
            for part in range(2):
                gift_out[section, part] = joined(section, part).astype(f32)
            gifts[section].start()
        perm_load.wait()
        row_load.wait()
        owner_load.wait()
        swapped = jnp.broadcast_to(owner[0:1, 0:1], (rank, rows)) != line
        rows_out[0] = jnp.where(swapped, row[1].astype(f32), row[0].astype(f32))
        give_rows(0).start()
        rows_out[1] = jnp.where(swapped, row[0].astype(f32), row[1].astype(f32))

        @pl.when(jnp.logical_not(bottom))
        def _():
            give_rows(1).start()

        for n in range(leaves):
            diagonal(n)

        @pl.when(bottom)
        def _():
            word(2, g, b).wait_recv()
            sent = word_in[2].astype(bf16)
            pl.semaphore_wait(ready, 1)
            for c in range(CHUNKS):
                outgoing[1, c] = jnp.dot(
                    sent, row[...].reshape(both, rows)[:, c * size:(c + 1) * size],
                    preferred_element_type=f32,
                )
                inward(c, sibling).start()

        give_rows(0).wait_recv()
        rows_low[:rank] = rows_in[0].astype(bf16)

        @pl.when(top)
        def _():
            rows_low[rank:] = jnp.zeros((rank, rows), bf16)
            for c in range(CHUNKS):
                shift(1, c).wait_recv()
                out_ref[:, c * size:(c + 1) * size] += incoming[1, c]
            word(0, g, b).wait_recv()
            word_in[1] = jnp.zeros((vectors, both), f32)

        @pl.when(jnp.logical_not(top))
        def _():
            give_rows(1).wait_recv()
            rows_low[rank:] = rows_in[1].astype(bf16)
            word(0, g, b).wait_recv()
            word(1, g, b).wait_recv()

        final = (word_in[0] + word_in[1]).astype(bf16)
        for c in range(CHUNKS):
            where = slice(c * size, (c + 1) * size)
            out_ref[:, where] += jnp.dot(final, rows_low[:, where], preferred_element_type=f32)

        seed.wait_send()
        for gift in gifts:
            gift.wait_send()
        loan.wait_send()
        give_rows(0).wait_send()

        @pl.when(jnp.logical_not(bottom))
        def _():
            give_rows(1).wait_send()

        @pl.when(bottom)
        def _():
            for c in range(CHUNKS):
                inward(c, sibling).wait_send()

    @pl.when(core == 1)
    def _():
        greet(g, flip(second, 0))
        for friend in (second, third, fourth, cross):
            greet(g, friend)

        zero = jnp.zeros((rank, rank), bf16)

        def place(j, section, part, made):
            for level in range(levels):
                wide = [zero] * levels
                wide[level] = made(level)
                start = part * both + level * rank
                weights[j, section, start:start + rank, :] = jnp.concatenate(wide, axis=1)

        def gift_of(section, part):
            return lambda level: gift_in[section, part, :, level * rank:(level + 1) * rank].astype(bf16)

        def mix_of(section, part):
            return lambda level: mix[0, level, section, part]

        def reordered(made):
            index = lax.broadcasted_iota(jnp.int32, (rank, rank), 0)
            return lambda level: jnp.dot(
                jnp.where(index == perm[level:level + 1, :], 1.0, 0.0).astype(bf16), made(level),
                preferred_element_type=f32,
            ).astype(bf16)

        def post(slot, target):
            return remote(
                mail_out.at[slot], mail_in.at[slot], mail_send.at[slot], mail_recv.at[slot], g, target
            )

        own = project()
        mix_load.wait()
        lent[...] = joined(1, 1).astype(f32)
        meet(7, 2, 2)

        @pl.when(top)
        def _():
            for member in (b, sibling):
                pl.semaphore_signal(ready, inc=1, device_id=(up, member), device_id_type=MESH)

        loan = lend(1, second)
        loan.start()
        perm_load.wait()
        for part in range(2):
            place(1, 0, part, reordered(mix_of(0, part)))
        place(1, 1, 0, mix_of(1, 0))
        gifts[0].wait_recv()
        for part in range(2):
            place(0, 0, part, reordered(gift_of(0, part)))
        seed.wait_recv()
        pair = [seed_in[...], own]
        state = [
            split_dot(jnp.concatenate([pair[j], pair[1 - j]], axis=1), weights[j, 0]) for j in range(2)
        ]

        for j in range(2):
            mail_out[RAW, j] = state[j]
        raw = post(RAW, second)
        raw.start()
        gifts[1].wait_recv()
        place(0, 1, 0, gift_of(1, 0))
        mine = [split_dot(state[j], weights[j, 1, :both]) for j in range(2)]
        for j in range(2):
            mail_out[DIRECT, j] = mine[j]
        direct = post(DIRECT, third)
        direct.start()
        for j in range(2):
            lend(j, b).wait_recv()
            place(j, sections, 0, lambda level: borrowed[j, :, level * rank:(level + 1) * rank].astype(bf16))
        for j in range(2):
            mail_out[DETOUR, j] = split_dot(state[j], weights[j, sections, :both])
        detour = post(DETOUR, cross)
        detour.start()
        place(0, 1, 1, gift_of(1, 1))
        place(1, 1, 1, mix_of(1, 1))
        for section in (2, 3):
            gifts[section].wait_recv()
            for part in range(2):
                place(0, section, part, gift_of(section, part))
                place(1, section, part, mix_of(section, part))
        diagonal(0)
        diagonal(1)
        raw.wait_recv()
        state = [mine[j] + split_dot(mail_in[RAW, j], weights[j, 1, both:]) for j in range(2)]
        mine = [split_dot(state[j], weights[j, 2, :both]) for j in range(2)]
        detour.wait_recv()
        direct.wait_recv()
        state = [
            mine[j] + split_dot(mail_in[DIRECT, j] + mail_in[DETOUR, j], weights[j, 2, both:])
            for j in range(2)
        ]
        for j in range(2):
            mail_out[LAST, j] = state[j]
        last = post(LAST, fourth)
        last.start()
        mine = [split_dot(state[j], weights[j, 3, :both]) for j in range(2)]
        for n in range(2, leaves):
            diagonal(n)
        row_load.wait()
        owner_load.wait()
        lane_level = lax.broadcasted_iota(jnp.int32, (vectors, both), 1) // rank
        swapped = jnp.broadcast_to(owner[0:1, 0:1], (vectors, both)) != line
        to_half = lane_level == jnp.where(swapped, 1, 0)
        last.wait_recv()
        state = [mine[j] + split_dot(mail_in[LAST, j], weights[j, 3, both:]) for j in range(2)]

        told = state[0].astype(bf16).astype(f32)
        ordered = jnp.where(swapped, pltpu.roll(told, rank, 1), told)
        word_out[0] = jnp.where(lane_level == 0, ordered, 0.0)
        word(0, half, sibling).start()

        @pl.when(bottom)
        def _():
            word_out[2] = jnp.where(to_half, 0.0, told)
            word(2, g, sibling).start()

        @pl.when(jnp.logical_not(bottom))
        def _():
            word_out[1] = jnp.where(lane_level == 0, 0.0, ordered)
            word(1, down, sibling).start()

        sent = jnp.concatenate(
            [jnp.where(to_half, state[1], 0.0), jnp.where(to_half, 0.0, state[1])], axis=0
        ).astype(bf16)
        factor = row[...].reshape(both, rows)

        @pl.when(bottom)
        def _():
            pl.semaphore_wait(ready, 1)

        for c in range(CHUNKS):
            where = slice(c * size, (c + 1) * size)
            block = jnp.dot(sent, factor[:, where], preferred_element_type=f32)
            outgoing[0, c] = block[:vectors]
            outgoing[1, c] = block[vectors:]
            shift(1, c).start()

            @pl.when(jnp.logical_not(top))
            def _():
                shift(0, c).start()

        @pl.when(top)
        def _():
            for c in range(CHUNKS):
                shift(1, c).wait_recv()
                outgoing[0, c] += incoming[1, c]
                shift(0, c).start()
            for c in range(CHUNKS):
                inward(c, b).wait_recv()
                onward(c).start()

        for c in range(CHUNKS):
            where = slice(c * size, (c + 1) * size)
            shift(0, c).wait_recv()

            @pl.when(top)
            def _():
                out_ref[:, where] += incoming[0, c]

            @pl.when(jnp.logical_not(top))
            def _():
                shift(1, c).wait_recv()
                out_ref[:, where] += incoming[0, c] + incoming[1, c]

        for copy in (loan, raw, direct, detour, last):
            copy.wait_send()
        word(0, half, sibling).wait_send()

        @pl.when(bottom)
        def _():
            word(2, g, sibling).wait_send()

        @pl.when(jnp.logical_not(bottom))
        def _():
            word(1, down, sibling).wait_send()

        for c in range(CHUNKS):
            for way in range(2):
                shift(way, c).wait_send()

        @pl.when(top)
        def _():
            for c in range(CHUNKS):
                onward(c).wait_send()


def shards(field, leaf_inverse, col_factor, row_factor, mixing, row_owner, rank_perm):
    vectors, rows = field.shape
    levels, rank, _ = col_factor.shape
    sections = mixing.shape[2]
    both = levels * rank
    f32, bf16 = jnp.float32, jnp.bfloat16
    args = (field, leaf_inverse, col_factor, row_factor, mixing, row_owner, rank_perm)
    args = [pltpu.with_memory_space_constraint(x, pltpu.HBM) for x in args]
    dma = pltpu.SemaphoreType.DMA
    return pl.pallas_call(
        kernel,
        out_shape=pltpu.VMEM((vectors, rows), f32),
        in_specs=[pl.BlockSpec(memory_space=pltpu.HBM)] * len(args),
        out_specs=pl.BlockSpec(memory_space=pltpu.VMEM),
        scratch_shapes=[
            pltpu.VMEM(field.shape, f32),
            pltpu.VMEM(leaf_inverse.shape, bf16),
            pltpu.VMEM(col_factor.shape, bf16),
            pltpu.VMEM(row_factor.shape, bf16),
            pltpu.VMEM(mixing.shape, bf16),
            pltpu.VMEM(row_owner.shape, jnp.int32),
            pltpu.VMEM(rank_perm.shape, jnp.int32),
            pltpu.VMEM((2, sections + 1, 2 * both, both), bf16),
            pltpu.VMEM((vectors, both), f32),
            pltpu.VMEM((vectors, both), f32),
            pltpu.VMEM((sections, 2, rank, both), f32),
            pltpu.VMEM((sections, 2, rank, both), f32),
            pltpu.VMEM((rank, both), f32),
            pltpu.VMEM((2, rank, both), f32),
            pltpu.VMEM((4, 2, vectors, both), f32),
            pltpu.VMEM((4, 2, vectors, both), f32),
            pltpu.VMEM((3, vectors, both), f32),
            pltpu.VMEM((3, vectors, both), f32),
            pltpu.VMEM((2, rank, rows), f32),
            pltpu.VMEM((2, rank, rows), f32),
            pltpu.VMEM((both, rows), bf16),
            pltpu.VMEM((2, CHUNKS, vectors, rows // CHUNKS), f32),
            pltpu.VMEM((2, CHUNKS, vectors, rows // CHUNKS), f32),
            pltpu.VMEM((CHUNKS, vectors, rows // CHUNKS), f32),
            dma((6,)), dma((leaf_inverse.shape[0],)), dma((2,)), dma((sections,)), dma((sections,)),
            dma((1,)), dma((2,)), dma((4,)), dma((4,)), dma((3,)), dma((3,)), dma((2,)), dma((2,)),
            dma((2, CHUNKS)), dma((2, CHUNKS)), dma((CHUNKS,)), dma((CHUNKS,)),
            pltpu.SemaphoreType.REGULAR,
        ],
        compiler_params=pltpu.CompilerParams(
            collective_id=0, has_side_effects=True, vmem_limit_bytes=60 * 2**20
        ),
    )(*args)


def solution(mesh):
    in_specs = (
        P(None, ("grp", "bf")),
        P(("grp", "bf"), None, None),
        P(None, None, ("grp", "bf")),
        P(None, None, ("grp", "bf")),
        P(("grp", "bf"), None, None, None, None, None),
        P(),
        P(),
    )
    out_specs = P(None, ("grp", "bf"))
    return jax.shard_map(shards, mesh=mesh, in_specs=in_specs, out_specs=out_specs, check_vma=False)
```

time: 120 us -> 19.2 us (0.16)
  the two profiles are of different devices: /device:TPU:8 before, /device:TPU:97 now
where the time goes in v3:
time: 19.2 us
  Pallas kernels  18.5 us (96%)
  local copies, waits for them, and re-layouts  0.66 us (3%)
    pallas_call x1, Pallas kernels, shards(): pl.pallas_call(kernel, out_shape=pltpu.VMEM((vectors, rows), f32), in_spe...  18.5 us
    unnamed x1, local copies, waits for them, and re-layouts  0.66 us

profile of v3, /device:TPU:97, one launch (start us, length us, event | category | flops | bytes accessed | tf_op | source)
XLA Modules:
  0.0 19.2 jit_solution(7293882188122985635)
XLA Ops:
  0.0 18.5 %shard_map.73 = f32[16,2048]{1,0:T(8,128)S(1)} custom-call(f32[16,2048]{1,0:T(8,128)} %field_hbm.1, bf16[4,512,512]{2,1,0:T(8,128)(2,1)} %leaf_hbm.1, bf16[2,64,2048]{2,1,0:T(8,128)(2,1)} %col_hbm.1, bf16[2,64,2048]{2,1,0:T(8,128)(2,1)} %row_hbm.1, bf16[1,2,4,2,64,64]{5,4,3,2,1,0:T(8,128)(2,1)} %mix_hbm.1, s32[2,16]{1,0:T(2,128)} %owner_hbm.1, s32[2,64]{1,0:T(2,128)} %perm_hbm.1), custom_call_target="tpu_custom_call" | custom-call | tf_op jit(solution)/shard_map/pallas_call | solution.py:435
  18.5 0.7 %copy.9 = f32[16,2048]{1,0:T(8,128)} copy(f32[16,2048]{1,0:T(8,128)S(1)} %shard_map.73) | data formatting | bytes 262144

commit v4 on v3

v4 whole, which is shorter than its diff:
```python
import jax
import jax.numpy as jnp
from jax import lax
from jax.experimental import pallas as pl
from jax.experimental.pallas import tpu as pltpu
from jax.sharding import PartitionSpec as P

MESH = pl.DeviceIdType.MESH
AHEAD = 3, 8
PIECES = 2
RAW, DIRECT, DETOUR, LAST = range(4)
GIFTS = ((1, 1), (0, 0), (0, 1), (1, 0), (2, 0), (2, 1), (3, 0), (3, 1))


def split_dot(lhs, weights):
    high = lhs.astype(jnp.bfloat16)
    low = (lhs - high.astype(jnp.float32)).astype(jnp.bfloat16)
    both = jnp.dot(
        jnp.concatenate([high, low], axis=0), weights, preferred_element_type=jnp.float32
    )
    rows = lhs.shape[0]
    return both[:rows] + both[rows:]


def flip(index, bit):
    step = 2**bit
    return index + step - 2 * step * ((index // step) % 2)


def kernel(
    field_hbm, leaf_hbm, col_hbm, row_hbm, mix_hbm, owner_hbm, perm_hbm,
    out_ref,
    field, leaf, col, row, mix, owner, perm, weights,
    seed_out, seed_in, gift_out, gift_in, lent, borrowed, mail_out, mail_in,
    word_out, word_in, rows_out, rows_in, ahead_out, ahead_held, ahead_in, rows_low,
    out_first, out_rest, in_first, in_rest, relay_first, relay_rest,
    load_sem, leaf_sem, seed_sem, gift_send, gift_recv, lend_send, lend_recv, mail_send, mail_recv,
    word_send, word_recv, rows_send, rows_recv, held_send, held_recv, ahead_send, ahead_recv, shift_send, shift_recv, relay_send, relay_recv, ready, go,
):
    g, b = lax.axis_index("grp"), lax.axis_index("bf")
    groups = lax.axis_size("grp")
    vectors, rows = field.shape
    levels, rank, _ = col.shape
    leaves, order, _ = leaf.shape
    sections = mix.shape[2]
    both = levels * rank
    ahead = out_first.shape[2]
    pieces = (slice(0, ahead), slice(ahead, rows))
    outgoing, incoming, relay = (out_first, out_rest), (in_first, in_rest), (relay_first, relay_rest)
    f32, bf16 = jnp.float32, jnp.bfloat16

    def load(i, src, dst):
        copy = pltpu.make_async_copy(src, dst, load_sem.at[i])
        copy.start()
        return copy

    half_mix = sections // 2
    mix_load = load(3, mix_hbm.at[:, :, :half_mix], mix.at[:, :, :half_mix])
    perm_load = load(2, perm_hbm, perm)
    field_load = load(0, field_hbm, field)
    col_load = load(1, col_hbm, col)
    rest_load = load(6, mix_hbm.at[:, :, half_mix:], mix.at[:, :, half_mix:])

    line, core = groups // 2, b % 2
    z = g % line
    half, down, up = (g + line) % groups, g - z + (z + line - 1) % line, g - z + (z + 1) % line
    sibling, second, third, fourth = (flip(b, bit) for bit in range(4))
    cross = flip(second, 2)
    bottom, top = z == 0, z == line - 1
    barrier = pltpu.get_barrier_semaphore()

    def greet(group, member):
        pl.semaphore_signal(barrier, inc=1, device_id=(group, member), device_id_type=MESH)

    greet(g, sibling)
    greet(half, b + 1 - core)

    @pl.when(jnp.logical_not(top))
    def _():
        greet(up, b + 1 - core)

    @pl.when(bottom)
    def _():
        greet(down, b + 1 - core)

    @pl.when(core == 1)
    def _():
        for friend in (third, fourth, second, cross):
            greet(g, friend)

    owner_load = load(5, owner_hbm, owner)
    row_load = load(4, row_hbm, row)
    leaf_loads = [
        pltpu.make_async_copy(leaf_hbm.at[n], leaf.at[n], leaf_sem.at[n]) for n in range(leaves)
    ]
    for copy in leaf_loads:
        copy.start()

    def remote(src, dst, send, recv, group, member):
        return pltpu.make_async_remote_copy(
            src_ref=src, dst_ref=dst, send_sem=send, recv_sem=recv,
            device_id=(group, member), device_id_type=MESH,
        )

    seed = remote(seed_out, seed_in, seed_sem.at[0], seed_sem.at[1], g, sibling)
    gifts = [
        remote(gift_out.at[part], gift_in.at[part], gift_send.at[i], gift_recv.at[i], g, sibling)
        for i, part in enumerate((pl.ds(0, 4), pl.ds(4, 4)))
    ]

    def lend(j, source):
        return remote(source, borrowed.at[j], lend_send.at[j], lend_recv.at[j], g, third)

    def shift(way, c):
        return remote(
            outgoing[c].at[way], incoming[c].at[way], shift_send.at[way, c], shift_recv.at[way, c],
            (half, down)[way], b,
        )

    def inward(c, member):
        return remote(
            outgoing[c].at[1], relay[c], shift_send.at[1, c], relay_recv.at[c], down, member
        )

    def onward(c):
        return remote(
            relay[c], incoming[c].at[1], relay_send.at[c], shift_recv.at[1, c], half, sibling
        )

    def word(i, group, member):
        return remote(word_out.at[i], word_in.at[i], word_send.at[i], word_recv.at[i], group, member)

    def give_rows(way):
        return remote(
            rows_out.at[way], rows_in.at[way], rows_send.at[way], rows_recv.at[way],
            (half, down)[way], b,
        )

    def hold(way):
        return remote(
            ahead_out.at[way], ahead_held.at[way], held_send.at[way], held_recv.at[way], g, sibling
        )

    def give_ahead(way, member):
        return remote(
            ahead_held.at[way], ahead_in.at[way], ahead_send.at[way], ahead_recv.at[way],
            (half, down)[way], member,
        )

    def by_way(width):
        swapped = jnp.broadcast_to(owner[0:1, 0:1], (rank, width)) != line
        first, other = row[0, :, :width].astype(f32), row[1, :, :width].astype(f32)
        return jnp.where(swapped, other, first), jnp.where(swapped, first, other)

    def factor_of(section, part):
        def made(level):
            block = mix[0, level, section, part]
            if section:
                return block
            index = lax.broadcasted_iota(jnp.int32, (rank, rank), 0)
            chosen = jnp.where(index == perm[level:level + 1, :], 1.0, 0.0).astype(bf16)
            return jnp.dot(chosen, block, preferred_element_type=f32).astype(bf16)

        return made

    def joined(section, part):
        made = factor_of(section, part)
        return jnp.concatenate([made(level) for level in range(levels)], axis=1).astype(f32)

    def project():
        field_load.wait()
        col_load.wait()
        return lax.dot_general(
            field[...].astype(bf16), col[...].reshape(both, rows), (((1,), (1,)), ((), ())),
            preferred_element_type=f32,
        )

    def diagonal(n):
        leaf_loads[n].wait()
        where = slice(n * order, (n + 1) * order)
        out_ref[:, where] = jnp.dot(
            field[:, where].astype(bf16), leaf[n], preferred_element_type=f32
        )

    @pl.when(core == 0)
    def _():
        mix_load.wait()
        perm_load.wait()
        for i, (section, part) in enumerate(GIFTS[:4]):
            gift_out[i] = joined(section, part)
        pl.semaphore_wait(barrier, 1)
        gifts[0].start()
        seed_out[...] = project()
        seed.start()
        rest_load.wait()
        for i, (section, part) in enumerate(GIFTS[4:], 4):
            gift_out[i] = joined(section, part)
        gifts[1].start()
        row_load.wait()
        owner_load.wait()
        rows_out[0], rows_out[1] = by_way(rows)

        pl.semaphore_wait(go, 1)
        give_rows(0).start()

        @pl.when(jnp.logical_not(bottom))
        def _():
            give_rows(1).start()

        @pl.when(jnp.logical_not(bottom))
        def _():
            hold(1).wait_recv()
            give_ahead(1, sibling).start()

        @pl.when(jnp.logical_not(top))
        def _():
            hold(0).wait_recv()
            give_ahead(0, sibling).start()

        for n in range(leaves):
            diagonal(n)

        @pl.when(bottom)
        def _():
            word(4, g, b).wait_recv()
            sent = word_in[4].astype(bf16)
            pl.semaphore_wait(ready, 1)
            for c, where in enumerate(pieces):
                outgoing[c][1] = jnp.dot(
                    sent, row[...].reshape(both, rows)[:, where], preferred_element_type=f32
                )
                inward(c, sibling).start()

        give_rows(0).wait_recv()
        rows_low[:rank] = rows_in[0].astype(bf16)

        @pl.when(top)
        def _():
            rows_low[rank:] = jnp.zeros((rank, rows), bf16)
            word_in[1] = jnp.zeros((vectors, both), f32)

        @pl.when(jnp.logical_not(top))
        def _():
            give_rows(1).wait_recv()
            rows_low[rank:] = rows_in[1].astype(bf16)
            word(1, g, b).wait_recv()

        word(0, g, b).wait_recv()
        final = (word_in[0] + word_in[1]).astype(bf16)
        out_ref[...] += jnp.dot(final, rows_low[...], preferred_element_type=f32)

        @pl.when(top)
        def _():
            for c, where in enumerate(pieces):
                shift(1, c).wait_recv()
                out_ref[:, where] += incoming[c][1]

        seed.wait_send()
        for gift in gifts:
            gift.wait_send()
        give_rows(0).wait_send()

        @pl.when(jnp.logical_not(bottom))
        def _():
            give_rows(1).wait_send()
            give_ahead(1, sibling).wait_send()

        @pl.when(jnp.logical_not(top))
        def _():
            give_ahead(0, sibling).wait_send()

        @pl.when(bottom)
        def _():
            for c in range(PIECES):
                inward(c, sibling).wait_send()

    @pl.when(core == 1)
    def _():
        zero = jnp.zeros((rank, rank), bf16)

        def place(j, section, part, made):
            for level in range(levels):
                wide = [zero] * levels
                wide[level] = made(level)
                start = part * both + level * rank
                weights[j, section, start:start + rank, :] = jnp.concatenate(wide, axis=1)

        def gift_of(section, part):
            i = GIFTS.index((section, part))
            return lambda level: gift_in[i, :, level * rank:(level + 1) * rank].astype(bf16)

        def post(kept, slot, target):
            return remote(
                mail_out.at[kept], mail_in.at[slot], mail_send.at[slot], mail_recv.at[slot], g, target
            )

        mix_load.wait()
        perm_load.wait()
        lent[...] = joined(1, 1)
        for part in range(2):
            place(1, 0, part, factor_of(0, part))
        place(1, 1, 0, factor_of(1, 0))
        own = project()
        pl.semaphore_wait(barrier, 7 + jnp.where(bottom, 0, 2) + jnp.where(top, 2, 0))
        loans = [lend(0, gift_in.at[0]), lend(1, lent)]
        loans[1].start()
        pl.semaphore_signal(go, inc=1, device_id=(g, sibling), device_id_type=MESH)

        @pl.when(top)
        def _():
            for member in (b, sibling):
                pl.semaphore_signal(ready, inc=1, device_id=(up, member), device_id_type=MESH)

        gifts[0].wait_recv()
        loans[0].start()
        for part in range(2):
            place(0, 0, part, gift_of(0, part))
        place(0, 1, 0, gift_of(1, 0))
        seed.wait_recv()
        pair = [seed_in[...], own]
        state = [
            split_dot(jnp.concatenate([pair[j], pair[1 - j]], axis=1), weights[j, 0]) for j in range(2)
        ]

        raw, detour = post(RAW, RAW, second), post(RAW, DETOUR, cross)
        direct = post(DIRECT, DIRECT, third)
        mine = [split_dot(state[j], weights[j, 1, :both]) for j in range(2)]
        for j in range(2):
            mail_out[RAW, j] = state[j]
            mail_out[DIRECT, j] = mine[j]
        direct.start()
        detour.start()
        raw.start()
        place(0, 1, 1, gift_of(1, 1))
        place(1, 1, 1, factor_of(1, 1))
        rest_load.wait()
        gifts[1].wait_recv()
        for section in (2, 3):
            for part in range(2):
                place(0, section, part, gift_of(section, part))
                place(1, section, part, factor_of(section, part))
        row_load.wait()
        owner_load.wait()
        ahead_out[0], ahead_out[1] = by_way(ahead)

        @pl.when(jnp.logical_not(bottom))
        def _():
            hold(1).start()

        @pl.when(jnp.logical_not(top))
        def _():
            hold(0).start()

        diagonal(0)
        diagonal(1)
        raw.wait_recv()
        state = [mine[j] + split_dot(mail_in[RAW, j], weights[j, 1, both:]) for j in range(2)]
        mine = [split_dot(state[j], weights[j, 2, :both]) for j in range(2)]
        detour.wait_recv()
        for j in range(2):
            loans[j].wait_recv()
            place(j, sections, 0, lambda level: borrowed[j, :, level * rank:(level + 1) * rank].astype(bf16))
        far = [split_dot(mail_in[DETOUR, j], weights[j, sections, :both]) for j in range(2)]
        direct.wait_recv()
        state = [
            mine[j] + split_dot(mail_in[DIRECT, j] + far[j], weights[j, 2, both:]) for j in range(2)
        ]
        for j in range(2):
            mail_out[LAST, j] = state[j]
        last = post(LAST, LAST, fourth)
        last.start()
        mine = [split_dot(state[j], weights[j, 3, :both]) for j in range(2)]
        for n in range(2, leaves):
            diagonal(n)
        lane_level = lax.broadcasted_iota(jnp.int32, (vectors, both), 1) // rank
        swapped = jnp.broadcast_to(owner[0:1, 0:1], (vectors, both)) != line
        to_half = lane_level == jnp.where(swapped, 1, 0)
        last.wait_recv()
        state = [mine[j] + split_dot(mail_in[LAST, j], weights[j, 3, both:]) for j in range(2)]

        told = [state[j].astype(bf16).astype(f32) for j in range(2)]
        ordered = [jnp.where(swapped, pltpu.roll(told[j], rank, 1), told[j]) for j in range(2)]
        for j in range(2):
            word_out[2 * j] = jnp.where(lane_level == 0, ordered[j], 0.0)
            word_out[2 * j + 1] = jnp.where(lane_level == 0, 0.0, ordered[j])
        word_out[4] = jnp.where(to_half, 0.0, told[0])
        sent = jnp.concatenate(
            [jnp.where(to_half, told[1], 0.0), jnp.where(to_half, 0.0, told[1])], axis=0
        ).astype(bf16)
        factor = row[...].reshape(both, rows)

        def make(c):
            block = jnp.dot(sent, factor[:, pieces[c]], preferred_element_type=f32)
            outgoing[c][0] = block[:vectors]
            outgoing[c][1] = block[vectors:]

        @pl.when(bottom)
        def _():
            word(4, g, sibling).start()

        @pl.when(jnp.logical_not(bottom))
        def _():
            word(1, down, sibling).start()
            word(3, down, b).start()

        word(0, half, sibling).start()

        @pl.when(jnp.logical_not(top))
        def _():
            word(2, half, b).start()

        make(1)

        @pl.when(jnp.logical_not(bottom))
        def _():
            shift(1, 1).start()

        @pl.when(jnp.logical_not(top))
        def _():
            shift(0, 1).start()

        @pl.when(bottom)
        def _():
            make(0)
            pl.semaphore_wait(ready, 1)
            for c in range(PIECES):
                shift(1, c).start()

        @pl.when(top)
        def _():
            make(0)
            for c, where in enumerate(pieces):
                shift(1, c).wait_recv()
                outgoing[c][0] += incoming[c][1]
                shift(0, c).start()
            for c in range(PIECES):
                inward(c, b).wait_recv()
                onward(c).start()
            for c, where in enumerate(pieces):
                shift(0, c).wait_recv()
                out_ref[:, where] += incoming[c][0]

        @pl.when(jnp.logical_not(top))
        def _():
            for way in (1, 0):
                give_ahead(way, b).wait_recv()
                rows_low[way * rank:(way + 1) * rank, :ahead] = ahead_in[way].astype(bf16)
                word(2 + way, g, b).wait_recv()
            final = (word_in[2] + word_in[3]).astype(bf16)
            out_ref[:, :ahead] += jnp.dot(final, rows_low[:, :ahead], preferred_element_type=f32)
            for way in (1, 0):
                shift(way, 1).wait_recv()
            out_ref[:, ahead:] += incoming[1][0] + incoming[1][1]

        for copy in (*loans, raw, direct, detour, last):
            copy.wait_send()
        word(0, half, sibling).wait_send()
        for way in range(2):
            shift(way, 1).wait_send()

        @pl.when(bottom)
        def _():
            word(4, g, sibling).wait_send()
            shift(1, 0).wait_send()

        @pl.when(jnp.logical_not(bottom))
        def _():
            hold(1).wait_send()
            word(1, down, sibling).wait_send()
            word(3, down, b).wait_send()

        @pl.when(top)
        def _():
            shift(0, 0).wait_send()
            for c in range(PIECES):
                onward(c).wait_send()

        @pl.when(jnp.logical_not(top))
        def _():
            hold(0).wait_send()
            word(2, half, b).wait_send()


def shards(field, leaf_inverse, col_factor, row_factor, mixing, row_owner, rank_perm):
    vectors, rows = field.shape
    levels, rank, _ = col_factor.shape
    sections = mixing.shape[2]
    both = levels * rank
    ahead = rows * AHEAD[0] // AHEAD[1]
    f32, bf16 = jnp.float32, jnp.bfloat16
    args = (field, leaf_inverse, col_factor, row_factor, mixing, row_owner, rank_perm)
    args = [pltpu.with_memory_space_constraint(x, pltpu.HBM) for x in args]
    dma = pltpu.SemaphoreType.DMA
    return pl.pallas_call(
        kernel,
        out_shape=pltpu.VMEM((vectors, rows), f32),
        in_specs=[pl.BlockSpec(memory_space=pltpu.HBM)] * len(args),
        out_specs=pl.BlockSpec(memory_space=pltpu.VMEM),
        scratch_shapes=[
            pltpu.VMEM(field.shape, f32),
            pltpu.VMEM(leaf_inverse.shape, bf16),
            pltpu.VMEM(col_factor.shape, bf16),
            pltpu.VMEM(row_factor.shape, bf16),
            pltpu.VMEM(mixing.shape, bf16),
            pltpu.VMEM(row_owner.shape, jnp.int32),
            pltpu.VMEM(rank_perm.shape, jnp.int32),
            pltpu.VMEM((2, sections + 1, 2 * both, both), bf16),
            pltpu.VMEM((vectors, both), f32),
            pltpu.VMEM((vectors, both), f32),
            pltpu.VMEM((2 * sections, rank, both), f32),
            pltpu.VMEM((2 * sections, rank, both), f32),
            pltpu.VMEM((rank, both), f32),
            pltpu.VMEM((2, rank, both), f32),
            pltpu.VMEM((4, 2, vectors, both), f32),
            pltpu.VMEM((4, 2, vectors, both), f32),
            pltpu.VMEM((5, vectors, both), f32),
            pltpu.VMEM((5, vectors, both), f32),
            pltpu.VMEM((2, rank, rows), f32),
            pltpu.VMEM((2, rank, rows), f32),
            pltpu.VMEM((2, rank, ahead), f32),
            pltpu.VMEM((2, rank, ahead), f32),
            pltpu.VMEM((2, rank, ahead), f32),
            pltpu.VMEM((both, rows), bf16),
            pltpu.VMEM((2, vectors, ahead), f32),
            pltpu.VMEM((2, vectors, rows - ahead), f32),
            pltpu.VMEM((2, vectors, ahead), f32),
            pltpu.VMEM((2, vectors, rows - ahead), f32),
            pltpu.VMEM((vectors, ahead), f32),
            pltpu.VMEM((vectors, rows - ahead), f32),
            dma((7,)), dma((leaf_inverse.shape[0],)), dma((2,)), dma((2,)), dma((2,)),
            dma((2,)), dma((2,)), dma((4,)), dma((4,)), dma((5,)), dma((5,)), dma((2,)), dma((2,)), dma((2,)), dma((2,)),
            dma((2,)), dma((2,)),
            dma((2, PIECES)), dma((2, PIECES)), dma((PIECES,)), dma((PIECES,)),
            pltpu.SemaphoreType.REGULAR, pltpu.SemaphoreType.REGULAR,
        ],
        compiler_params=pltpu.CompilerParams(
            collective_id=0, has_side_effects=True, vmem_limit_bytes=60 * 2**20
        ),
    )(*args)


def solution(mesh):
    in_specs = (
        P(None, ("grp", "bf")),
        P(("grp", "bf"), None, None),
        P(None, None, ("grp", "bf")),
        P(None, None, ("grp", "bf")),
        P(("grp", "bf"), None, None, None, None, None),
        P(),
        P(),
    )
    out_specs = P(None, ("grp", "bf"))
    return jax.shard_map(shards, mesh=mesh, in_specs=in_specs, out_specs=out_specs, check_vma=False)
```

time: 19.2 us -> 17.9 us (0.932)
  Pallas kernels: 18.5 us -> 17.1 us
    pallas_call x1, Pallas kernels: 18.5 us -> 17.1 us  [shards(): pl.pallas_call(kernel, out_shape=pltpu.VMEM((vectors, rows), f32), in_spe...]
where the time goes in v4:
time: 17.9 us; the launch traced here: 17.8 us
  Pallas kernels  17.1 us (96%)
  local copies, waits for them, and re-layouts  0.66 us (4%)
    pallas_call x1, Pallas kernels, shards(): pl.pallas_call(kernel, out_shape=pltpu.VMEM((vectors, rows), f32), in_spe...  17.1 us
    unnamed x1, local copies, waits for them, and re-layouts  0.66 us

profile of v4, /device:TPU:97, one launch (start us, length us, event | category | flops | bytes accessed | tf_op | source)
XLA Modules:
  0.0 17.8 jit_solution(7415326348640021381)
XLA Ops:
  0.0 17.1 %shard_map.73 = f32[16,2048]{1,0:T(8,128)S(1)} custom-call(f32[16,2048]{1,0:T(8,128)} %field_hbm.1, bf16[4,512,512]{2,1,0:T(8,128)(2,1)} %leaf_hbm.1, bf16[2,64,2048]{2,1,0:T(8,128)(2,1)} %col_hbm.1, bf16[2,64,2048]{2,1,0:T(8,128)(2,1)} %row_hbm.1, bf16[1,2,4,2,64,64]{5,4,3,2,1,0:T(8,128)(2,1)} %mix_hbm.1, s32[2,16]{1,0:T(2,128)} %owner_hbm.1, s32[2,64]{1,0:T(2,128)} %perm_hbm.1), custom_call_target="tpu_custom_call" | custom-call | tf_op jit(solution)/shard_map/pallas_call | solution.py:494
  17.2 0.7 %copy.9 = f32[16,2048]{1,0:T(8,128)} copy(f32[16,2048]{1,0:T(8,128)S(1)} %shard_map.73) | data formatting | bytes 262144

commit v5 on v4

--- a/solution.py
+++ b/solution.py
@@ -8,6 +8,7 @@
 MESH = pl.DeviceIdType.MESH
 AHEAD = 3, 8
 PIECES = 2
+STRIP = 16
 RAW, DIRECT, DETOUR, LAST = range(4)
 GIFTS = ((1, 1), (0, 0), (0, 1), (1, 0), (2, 0), (2, 1), (3, 0), (3, 1))
 
@@ -24,7 +25,7 @@
 
 def flip(index, bit):
     step = 2**bit
-    return index + step - 2 * step * ((index // step) % 2)
+    return index + step - 2 * step * lax.rem(lax.div(index, step), 2)
 
 
 def kernel(
@@ -54,6 +55,33 @@
         copy.start()
         return copy
 
+    line, core = groups // 2, lax.rem(b, 2)
+    z = lax.rem(g, line)
+    half, down, up = lax.rem(g + line, groups), g - z + lax.rem(z + line - 1, line), g - z + lax.rem(z + 1, line)
+    sibling, second, third, fourth = (flip(b, bit) for bit in range(4))
+    cross = flip(second, 2)
+    bottom, top = z == 0, z == line - 1
+    barrier = pltpu.get_barrier_semaphore()
+
+    def greet(group, member):
+        pl.semaphore_signal(barrier, inc=1, device_id=(group, member), device_id_type=MESH)
+
+    greet(half, b + 1 - core)
+
+    @pl.when(jnp.logical_not(top))
+    def _():
+        greet(up, b + 1 - core)
+
+    @pl.when(bottom)
+    def _():
+        greet(down, b + 1 - core)
+
+    @pl.when(core == 1)
+    def _():
+        for friend in (third, fourth, second, cross):
+            greet(g, friend)
+
+    greet(g, sibling)
     half_mix = sections // 2
     mix_load = load(3, mix_hbm.at[:, :, :half_mix], mix.at[:, :, :half_mix])
     perm_load = load(2, perm_hbm, perm)
@@ -61,40 +89,11 @@
     col_load = load(1, col_hbm, col)
     rest_load = load(6, mix_hbm.at[:, :, half_mix:], mix.at[:, :, half_mix:])
 
-    line, core = groups // 2, b % 2
-    z = g % line
-    half, down, up = (g + line) % groups, g - z + (z + line - 1) % line, g - z + (z + 1) % line
-    sibling, second, third, fourth = (flip(b, bit) for bit in range(4))
-    cross = flip(second, 2)
-    bottom, top = z == 0, z == line - 1
-    barrier = pltpu.get_barrier_semaphore()
-
-    def greet(group, member):
-        pl.semaphore_signal(barrier, inc=1, device_id=(group, member), device_id_type=MESH)
-
-    greet(g, sibling)
-    greet(half, b + 1 - core)
-
-    @pl.when(jnp.logical_not(top))
-    def _():
-        greet(up, b + 1 - core)
-
-    @pl.when(bottom)
-    def _():
-        greet(down, b + 1 - core)
-
-    @pl.when(core == 1)
-    def _():
-        for friend in (third, fourth, second, cross):
-            greet(g, friend)
-
     owner_load = load(5, owner_hbm, owner)
     row_load = load(4, row_hbm, row)
     leaf_loads = [
         pltpu.make_async_copy(leaf_hbm.at[n], leaf.at[n], leaf_sem.at[n]) for n in range(leaves)
     ]
-    for copy in leaf_loads:
-        copy.start()
 
     def remote(src, dst, send, recv, group, member):
         return pltpu.make_async_remote_copy(
@@ -105,7 +104,7 @@
     seed = remote(seed_out, seed_in, seed_sem.at[0], seed_sem.at[1], g, sibling)
     gifts = [
         remote(gift_out.at[part], gift_in.at[part], gift_send.at[i], gift_recv.at[i], g, sibling)
-        for i, part in enumerate((pl.ds(0, 4), pl.ds(4, 4)))
+        for i, part in enumerate((pl.ds(0, 1), pl.ds(1, 3), pl.ds(4, 4)))
     ]
 
     def lend(j, source):
@@ -147,25 +146,33 @@
             (half, down)[way], member,
         )
 
-    def by_way(width):
-        swapped = jnp.broadcast_to(owner[0:1, 0:1], (rank, width)) != line
-        first, other = row[0, :, :width].astype(f32), row[1, :, :width].astype(f32)
-        return jnp.where(swapped, other, first), jnp.where(swapped, first, other)
+    def by_way(into):
+        width = into.shape[2]
+        swapped = jnp.broadcast_to(owner[0:1, 0:1], (STRIP, width)) != line
+
+        def strip(i, carry):
+            where = pl.ds(pl.multiple_of(i * STRIP, STRIP), STRIP)
+            first, other = row[0, where, :width].astype(f32), row[1, where, :width].astype(f32)
+            into[0, where] = jnp.where(swapped, other, first)
+            into[1, where] = jnp.where(swapped, first, other)
+            return carry
+
+        lax.fori_loop(0, rank // STRIP, strip, 0)
+
+    def narrow(way, source, width):
+        def strip(i, carry):
+            where = pl.ds(pl.multiple_of(i * STRIP, STRIP), STRIP)
+            into = pl.ds(pl.multiple_of(way * rank + i * STRIP, STRIP), STRIP)
+            rows_low[into, :width] = source[way, where].astype(bf16)
+            return carry
+
+        lax.fori_loop(0, rank // STRIP, strip, 0)
 
     def factor_of(section, part):
-        def made(level):
-            block = mix[0, level, section, part]
-            if section:
-                return block
-            index = lax.broadcasted_iota(jnp.int32, (rank, rank), 0)
-            chosen = jnp.where(index == perm[level:level + 1, :], 1.0, 0.0).astype(bf16)
-            return jnp.dot(chosen, block, preferred_element_type=f32).astype(bf16)
-
-        return made
+        return lambda level: mix[0, level, section, part]
 
     def joined(section, part):
-        made = factor_of(section, part)
-        return jnp.concatenate([made(level) for level in range(levels)], axis=1).astype(f32)
+        return jnp.concatenate([mix[0, level, section, part] for level in range(levels)], axis=1).astype(f32)
 
     def project():
         field_load.wait()
@@ -176,29 +183,40 @@
         )
 
     def diagonal(n):
-        leaf_loads[n].wait()
-        where = slice(n * order, (n + 1) * order)
+        pltpu.make_async_copy(leaf_hbm.at[n], leaf.at[n], leaf_sem.at[n]).wait()
+        where = pl.ds(pl.multiple_of(n * order, order), order)
         out_ref[:, where] = jnp.dot(
             field[:, where].astype(bf16), leaf[n], preferred_element_type=f32
         )
+
+    def diagonals(start, stop):
+        def one(n, carry):
+            diagonal(n)
+            return carry
+
+        lax.fori_loop(start, stop, one, 0)
 
     @pl.when(core == 0)
     def _():
         mix_load.wait()
-        perm_load.wait()
-        for i, (section, part) in enumerate(GIFTS[:4]):
-            gift_out[i] = joined(section, part)
+        gift_out[0] = joined(*GIFTS[0])
         pl.semaphore_wait(barrier, 1)
         gifts[0].start()
+        for i, (section, part) in enumerate(GIFTS[1:4], 1):
+            gift_out[i] = joined(section, part)
+        gifts[1].start()
         seed_out[...] = project()
         seed.start()
+        for copy in leaf_loads:
+            copy.start()
         rest_load.wait()
         for i, (section, part) in enumerate(GIFTS[4:], 4):
             gift_out[i] = joined(section, part)
-        gifts[1].start()
+        gifts[2].start()
+        perm_load.wait()
         row_load.wait()
         owner_load.wait()
-        rows_out[0], rows_out[1] = by_way(rows)
+        by_way(rows_out)
 
         pl.semaphore_wait(go, 1)
         give_rows(0).start()
@@ -217,8 +235,7 @@
             hold(0).wait_recv()
             give_ahead(0, sibling).start()
 
-        for n in range(leaves):
-            diagonal(n)
+        diagonals(0, leaves)
 
         @pl.when(bottom)
         def _():
@@ -232,7 +249,7 @@
                 inward(c, sibling).start()
 
         give_rows(0).wait_recv()
-        rows_low[:rank] = rows_in[0].astype(bf16)
+        narrow(0, rows_in, rows)
 
         @pl.when(top)
         def _():
@@ -242,12 +259,18 @@
         @pl.when(jnp.logical_not(top))
         def _():
             give_rows(1).wait_recv()
-            rows_low[rank:] = rows_in[1].astype(bf16)
+            narrow(1, rows_in, rows)
             word(1, g, b).wait_recv()
 
         word(0, g, b).wait_recv()
         final = (word_in[0] + word_in[1]).astype(bf16)
-        out_ref[...] += jnp.dot(final, rows_low[...], preferred_element_type=f32)
+
+        def expand(n, carry):
+            where = pl.ds(pl.multiple_of(n * order, order), order)
+            out_ref[:, where] += jnp.dot(final, rows_low[:, where], preferred_element_type=f32)
+            return carry
+
+        lax.fori_loop(0, leaves, expand, 0)
 
         @pl.when(top)
         def _():
@@ -285,9 +308,21 @@
                 start = part * both + level * rank
                 weights[j, section, start:start + rank, :] = jnp.concatenate(wide, axis=1)
 
-        def gift_of(section, part):
-            i = GIFTS.index((section, part))
-            return lambda level: gift_in[i, :, level * rank:(level + 1) * rank].astype(bf16)
+        def spread(j, section, part, block):
+            shape = (both, both)
+            own_block = (
+                lax.broadcasted_iota(jnp.int32, shape, 0) // rank
+                == lax.broadcasted_iota(jnp.int32, shape, 1) // rank
+            )
+            weights[j, section, part * both:(part + 1) * both, :] = (
+                jnp.where(own_block, block, 0.0).astype(bf16)
+            )
+
+        def doubled(block):
+            return jnp.concatenate([block] * levels, axis=0)
+
+        def gift(section, part):
+            return gift_in[GIFTS.index((section, part))]
 
         def post(kept, slot, target):
             return remote(
@@ -297,10 +332,19 @@
         mix_load.wait()
         perm_load.wait()
         lent[...] = joined(1, 1)
+        index = lax.broadcasted_iota(jnp.int32, (rank, rank), 0)
+        chosen = jnp.concatenate(
+            [jnp.where(index == perm[level:level + 1, :], 1.0, 0.0) for level in range(levels)], axis=0
+        ).astype(bf16)
         for part in range(2):
-            place(1, 0, part, factor_of(0, part))
+            spread(1, 0, part, jnp.dot(chosen, joined(0, part).astype(bf16), preferred_element_type=f32))
         place(1, 1, 0, factor_of(1, 0))
         own = project()
+        for copy in leaf_loads:
+            copy.start()
+        row_load.wait()
+        owner_load.wait()
+        by_way(ahead_out)
         pl.semaphore_wait(barrier, 7 + jnp.where(bottom, 0, 2) + jnp.where(top, 2, 0))
         loans = [lend(0, gift_in.at[0]), lend(1, lent)]
         loans[1].start()
@@ -311,11 +355,20 @@
             for member in (b, sibling):
                 pl.semaphore_signal(ready, inc=1, device_id=(up, member), device_id_type=MESH)
 
+        @pl.when(jnp.logical_not(bottom))
+        def _():
+            hold(1).start()
+
+        @pl.when(jnp.logical_not(top))
+        def _():
+            hold(0).start()
+
         gifts[0].wait_recv()
         loans[0].start()
+        gifts[1].wait_recv()
         for part in range(2):
-            place(0, 0, part, gift_of(0, part))
-        place(0, 1, 0, gift_of(1, 0))
+            spread(0, 0, part, jnp.dot(chosen, gift(0, part).astype(bf16), preferred_element_type=f32))
+        spread(0, 1, 0, doubled(gift(1, 0)))
         seed.wait_recv()
         pair = [seed_in[...], own]
         state = [
@@ -324,42 +377,30 @@
 
         raw, detour = post(RAW, RAW, second), post(RAW, DETOUR, cross)
         direct = post(DIRECT, DIRECT, third)
+        for j in range(2):
+            mail_out[RAW, j] = state[j]
+        detour.start()
         mine = [split_dot(state[j], weights[j, 1, :both]) for j in range(2)]
         for j in range(2):
-            mail_out[RAW, j] = state[j]
             mail_out[DIRECT, j] = mine[j]
         direct.start()
-        detour.start()
         raw.start()
-        place(0, 1, 1, gift_of(1, 1))
+        spread(0, 1, 1, doubled(gift(1, 1)))
         place(1, 1, 1, factor_of(1, 1))
         rest_load.wait()
-        gifts[1].wait_recv()
+        gifts[2].wait_recv()
         for section in (2, 3):
             for part in range(2):
-                place(0, section, part, gift_of(section, part))
+                spread(0, section, part, doubled(gift(section, part)))
                 place(1, section, part, factor_of(section, part))
-        row_load.wait()
-        owner_load.wait()
-        ahead_out[0], ahead_out[1] = by_way(ahead)
-
-        @pl.when(jnp.logical_not(bottom))
-        def _():
-            hold(1).start()
-
-        @pl.when(jnp.logical_not(top))
-        def _():
-            hold(0).start()
-
-        diagonal(0)
-        diagonal(1)
+        diagonals(0, 2)
         raw.wait_recv()
         state = [mine[j] + split_dot(mail_in[RAW, j], weights[j, 1, both:]) for j in range(2)]
         mine = [split_dot(state[j], weights[j, 2, :both]) for j in range(2)]
         detour.wait_recv()
         for j in range(2):
             loans[j].wait_recv()
-            place(j, sections, 0, lambda level: borrowed[j, :, level * rank:(level + 1) * rank].astype(bf16))
+            spread(j, sections, 0, doubled(borrowed[j]))
         far = [split_dot(mail_in[DETOUR, j], weights[j, sections, :both]) for j in range(2)]
         direct.wait_recv()
         state = [
@@ -370,8 +411,7 @@
         last = post(LAST, LAST, fourth)
         last.start()
         mine = [split_dot(state[j], weights[j, 3, :both]) for j in range(2)]
-        for n in range(2, leaves):
-            diagonal(n)
+        diagonals(2, leaves)
         lane_level = lax.broadcasted_iota(jnp.int32, (vectors, both), 1) // rank
         swapped = jnp.broadcast_to(owner[0:1, 0:1], (vectors, both)) != line
         to_half = lane_level == jnp.where(swapped, 1, 0)
@@ -444,7 +484,7 @@
         def _():
             for way in (1, 0):
                 give_ahead(way, b).wait_recv()
-                rows_low[way * rank:(way + 1) * rank, :ahead] = ahead_in[way].astype(bf16)
+                narrow(way, ahead_in, ahead)
                 word(2 + way, g, b).wait_recv()
             final = (word_in[2] + word_in[3]).astype(bf16)
             out_ref[:, :ahead] += jnp.dot(final, rows_low[:, :ahead], preferred_element_type=f32)
@@ -527,7 +567,7 @@
             pltpu.VMEM((2, vectors, rows - ahead), f32),
             pltpu.VMEM((vectors, ahead), f32),
             pltpu.VMEM((vectors, rows - ahead), f32),
-            dma((7,)), dma((leaf_inverse.shape[0],)), dma((2,)), dma((2,)), dma((2,)),
+            dma((7,)), dma((leaf_inverse.shape[0],)), dma((2,)), dma((3,)), dma((3,)),
             dma((2,)), dma((2,)), dma((4,)), dma((4,)), dma((5,)), dma((5,)), dma((2,)), dma((2,)), dma((2,)), dma((2,)),
             dma((2,)), dma((2,)),
             dma((2, PIECES)), dma((2, PIECES)), dma((PIECES,)), dma((PIECES,)),

time: 17.9 us -> 17.8 us (level)
  no operation moved by 1% of the time
where the time goes in v5:
time: 17.8 us; the launch traced here: 17.7 us
  Pallas kernels  17.1 us (96%)
  local copies, waits for them, and re-layouts  0.66 us (4%)
    pallas_call x1, Pallas kernels, shards(): pl.pallas_call(kernel, out_shape=pltpu.VMEM((vectors, rows), f32), in_spe...  17.1 us
    unnamed x1, local copies, waits for them, and re-layouts  0.66 us

profile of v5, /device:TPU:97, one launch (start us, length us, event | category | flops | bytes accessed | tf_op | source)
XLA Modules:
  0.0 17.7 jit_solution(132459249713716826)
XLA Ops:
  0.0 17.1 %shard_map.73 = f32[16,2048]{1,0:T(8,128)S(1)} custom-call(f32[16,2048]{1,0:T(8,128)} %field_hbm.1, bf16[4,512,512]{2,1,0:T(8,128)(2,1)} %leaf_hbm.1, bf16[2,64,2048]{2,1,0:T(8,128)(2,1)} %col_hbm.1, bf16[2,64,2048]{2,1,0:T(8,128)(2,1)} %row_hbm.1, bf16[1,2,4,2,64,64]{5,4,3,2,1,0:T(8,128)(2,1)} %mix_hbm.1, s32[2,16]{1,0:T(2,128)} %owner_hbm.1, s32[2,64]{1,0:T(2,128)} %perm_hbm.1), custom_call_target="tpu_custom_call" | custom-call | tf_op jit(solution)/shard_map/pallas_call | solution.py:534
  17.1 0.7 %copy.9 = f32[16,2048]{1,0:T(8,128)} copy(f32[16,2048]{1,0:T(8,128)S(1)} %shard_map.73) | data formatting | bytes 262144

commit v6 on v5

--- a/solution.py
+++ b/solution.py
@@ -219,11 +219,12 @@
         by_way(rows_out)
 
         pl.semaphore_wait(go, 1)
+
+        @pl.when(jnp.logical_not(bottom))
+        def _():
+            give_rows(1).start()
+
         give_rows(0).start()
-
-        @pl.when(jnp.logical_not(bottom))
-        def _():
-            give_rows(1).start()
 
         @pl.when(jnp.logical_not(bottom))
         def _():
@@ -264,13 +265,7 @@
 
         word(0, g, b).wait_recv()
         final = (word_in[0] + word_in[1]).astype(bf16)
-
-        def expand(n, carry):
-            where = pl.ds(pl.multiple_of(n * order, order), order)
-            out_ref[:, where] += jnp.dot(final, rows_low[:, where], preferred_element_type=f32)
-            return carry
-
-        lax.fori_loop(0, leaves, expand, 0)
+        out_ref[...] += jnp.dot(final, rows_low[...], preferred_element_type=f32)
 
         @pl.when(top)
         def _():
@@ -347,8 +342,8 @@
         by_way(ahead_out)
         pl.semaphore_wait(barrier, 7 + jnp.where(bottom, 0, 2) + jnp.where(top, 2, 0))
         loans = [lend(0, gift_in.at[0]), lend(1, lent)]
+        pl.semaphore_signal(go, inc=1, device_id=(g, sibling), device_id_type=MESH)
         loans[1].start()
-        pl.semaphore_signal(go, inc=1, device_id=(g, sibling), device_id_type=MESH)
 
         @pl.when(top)
         def _():

time: 17.8 us -> 17.8 us (level)
  no operation moved by 1% of the time
where the time goes in v6:
time: 17.8 us; the launch traced here: 17.7 us
  Pallas kernels  17.1 us (96%)
  local copies, waits for them, and re-layouts  0.66 us (4%)
    pallas_call x1, Pallas kernels, shards(): pl.pallas_call(kernel, out_shape=pltpu.VMEM((vectors, rows), f32), in_spe...  17.1 us
    unnamed x1, local copies, waits for them, and re-layouts  0.66 us

profile of v6, /device:TPU:97, one launch (start us, length us, event | category | flops | bytes accessed | tf_op | source)
XLA Modules:
  0.0 17.7 jit_solution(14160664962946541853)
XLA Ops:
  0.0 17.1 %shard_map.73 = f32[16,2048]{1,0:T(8,128)S(1)} custom-call(f32[16,2048]{1,0:T(8,128)} %field_hbm.1, bf16[4,512,512]{2,1,0:T(8,128)(2,1)} %leaf_hbm.1, bf16[2,64,2048]{2,1,0:T(8,128)(2,1)} %col_hbm.1, bf16[2,64,2048]{2,1,0:T(8,128)(2,1)} %row_hbm.1, bf16[1,2,4,2,64,64]{5,4,3,2,1,0:T(8,128)(2,1)} %mix_hbm.1, s32[2,16]{1,0:T(2,128)} %owner_hbm.1, s32[2,64]{1,0:T(2,128)} %perm_hbm.1), custom_call_target="tpu_custom_call" | custom-call | tf_op jit(solution)/shard_map/pallas_call | solution.py:529
  17.1 0.7 %copy.9 = f32[16,2048]{1,0:T(8,128)} copy(f32[16,2048]{1,0:T(8,128)S(1)} %shard_map.73) | data formatting | bytes 262144
